TPU v7x, 256 devices: a whole 4x4x8 slice. The times are simulated.
256 devices in a mesh: gx: 32 (over x_lo, z, core), gz: 8 (over y, x_hi).
Axes of the slice: x: 4 (x_hi: 2, x_lo: 2; x = x_hi * 2 + x_lo), y: 4, z: 8, core: 2. Of those that a mesh axis runs over, the one named last changes fastest.
Arguments:
- velocity: float32 [3, 256, 256, 128], P(None, 'gx', 'gz'), may hold values from -12 to 12
- eddy_viscosity: float32 [4, 256, 256], P(None, 'gx', 'gz'), may hold values from 0.02 to 0.5
- target_spectrum: float32 [256], replicated, may hold values from 0.5 to 4
- mean_profile: float32 [128], replicated, may hold values from 0 to 2
- past_rewards: float32 [12, 256, 256], P(None, 'gx', 'gz'), may hold values from -6 to 6
- bootstrap_values: float32 [256, 256], P('gx', 'gz'), may hold values from -12 to 12
Outputs:
- final_velocity: float32 [3, 256, 256, 128], P(None, 'gx', 'gz')
- discounted_returns: float32 [16, 256, 256], P(None, 'gx', 'gz')
All inputs are finite; a program needn't handle non-finite values.
Results may differ from a plain program's by a relative error of at most 0.0001.
Values sent between devices are 32-bit elements; how exact they have to be, the bound alone decides.
A program may use at most 64 MiB of HBM per device.

v0:
```python
import math

import jax
import jax.numpy as jnp
from jax import lax
from jax.sharding import PartitionSpec as P

KX = 16
KZ = 16


step_length = 0.05
base_viscosity = 0.02
drive_force = 0.5
discount = 0.97


def padded_2(cells, sides, width):
    for axis, dim in sides:
        count = lax.axis_size(axis)
        head = lax.slice_in_dim(cells, 0, width, axis=dim)
        tail = lax.slice_in_dim(cells, cells.shape[dim] - width, cells.shape[dim], axis=dim)
        cells = jnp.concatenate(
            [
                lax.ppermute(tail, axis, [(i, (i + 1) % count) for i in range(count)]),
                cells,
                lax.ppermute(head, axis, [((i + 1) % count, i) for i in range(count)]),
            ],
            axis=dim,
        )
    return cells


def wall_shape(count):
    rows = jnp.arange(count).astype(jnp.float32) + 0.5
    return jnp.minimum(rows, count - rows) / (count / 2.0)


def phase_tables(waves, positions, total, factor):
    turns = jnp.arange(waves)[:, None] * positions[None, :] % total
    angle = turns.astype(jnp.float32) * (2.0 * math.pi / total)
    return (jnp.cos(angle) * factor, jnp.sin(angle) * factor)


def combine(center, x_plus, x_minus, z_plus, z_minus, viscous):
    padded = jnp.pad(center, ((0, 0), (0, 0), (0, 0), (1, 1)))
    y_plus = padded[:, :, :, 2:]
    y_minus = padded[:, :, :, :-2]
    grad_x = (x_plus - x_minus) * 0.5
    grad_z = (z_plus - z_minus) * 0.5
    grad_y = (y_plus - y_minus) * 0.5
    laplace = x_plus + x_minus + z_plus + z_minus + y_plus + y_minus - 6.0 * center
    carried = center[0][None] * grad_x + center[2][None] * grad_y + center[1][None] * grad_z
    forcing = jnp.array([drive_force, 0.0, 0.0], jnp.float32)[:, None, None, None]
    return -carried + viscous[None] * laplace + forcing


def halo_tendency(field, viscous):
    padded = padded_2(field, (("gx", 1), ("gz", 2)), 1)
    return combine(
        field,
        padded[:, 2:, 1:-1],
        padded[:, :-2, 1:-1],
        padded[:, 1:-1, 2:],
        padded[:, 1:-1, :-2],
        viscous,
    )


def advance(field, viscous):
    first = halo_tendency(field, viscous)
    second = halo_tendency(field + 0.5 * step_length * first, viscous)
    third = halo_tendency(field + 0.5 * step_length * second, viscous)
    fourth = halo_tendency(field + step_length * third, viscous)
    return field + step_length / 6.0 * (first + 2.0 * second + 2.0 * third + fourth)


def mode_sums(field, cos_x, sin_x, cos_z, sin_z):
    high = lax.Precision.HIGHEST
    part_c = jnp.einsum("kx,cxzy->kczy", cos_x, field, precision=high)
    part_s = jnp.einsum("kx,cxzy->kczy", sin_x, field, precision=high)
    real_part = jnp.einsum("kczy,lz->klcy", part_c, cos_z, precision=high) - jnp.einsum(
        "kczy,lz->klcy", part_s, sin_z, precision=high
    )
    imag_part = -(
        jnp.einsum("kczy,lz->klcy", part_s, cos_z, precision=high)
        + jnp.einsum("kczy,lz->klcy", part_c, sin_z, precision=high)
    )
    stacked = jnp.stack([real_part, imag_part], axis=2)
    return stacked.reshape(cos_x.shape[0] * cos_z.shape[0], 6, field.shape[3])


def spectral_terms(coefs, target):
    energy = jnp.sum(coefs * coefs, axis=(-2, -1)) / coefs.shape[-1]
    ratio = (energy - target) / (energy + target)
    return ratio * ratio


def on_device(
    velocity, eddy_viscosity, target_spectrum, mean_profile, past_rewards, bootstrap_values
):
    cells_x = velocity.shape[1]
    cells_z = velocity.shape[2]
    rows_y = velocity.shape[3]
    steps = eddy_viscosity.shape[0]
    total_x = cells_x * lax.axis_size("gx")
    total_z = cells_z * lax.axis_size("gz")
    factor = 1.0 / math.sqrt(total_x * total_z)
    x_spots = lax.axis_index("gx") * cells_x + jnp.arange(cells_x)
    z_spots = lax.axis_index("gz") * cells_z + jnp.arange(cells_z)
    cos_x, sin_x = phase_tables(KX, x_spots, total_x, factor)
    cos_z, sin_z = phase_tables(KZ, z_spots, total_z, 1.0)
    wall = wall_shape(rows_y)
    field = velocity
    locals_list = []
    spectra = []
    for step in range(steps):
        viscous = base_viscosity + eddy_viscosity[step][:, :, None] * wall[None, None, :]
        field = advance(field, viscous)
        offset = field[0] - mean_profile[None, None, :]
        locals_list.append(-jnp.mean(offset * offset, axis=2))
        coefs = mode_sums(field, cos_x, sin_x, cos_z, sin_z)
        summed = lax.psum(coefs, ("gx", "gz"))
        spectra.append(-jnp.sum(spectral_terms(summed, target_spectrum)) / KX)
    spectrum = jnp.stack(spectra)
    fresh = jnp.stack(locals_list) + spectrum[:, None, None]
    rewards = jnp.concatenate([past_rewards, fresh], axis=0)
    horizon = rewards.shape[0]
    running = bootstrap_values
    outputs = []
    for index in range(horizon - 1, -1, -1):
        running = rewards[index] + discount * running
        outputs.append(running)
    return (field, jnp.stack(outputs[::-1]))


def solution(mesh):
    placed = (
        P(None, "gx", "gz", None),
        P(None, "gx", "gz"),
        P(),
        P(),
        P(None, "gx", "gz"),
        P("gx", "gz"),
    )
    return jax.shard_map(
        on_device,
        mesh=mesh,
        in_specs=placed,
        out_specs=(P(None, "gx", "gz", None), P(None, "gx", "gz")),
        check_vma=False,
    )
```

profile of v0, /device:TPU:1, one launch (start us, length us, event | category | flops | bytes accessed | tf_op | source)
XLA Modules:
  0.0 546.9 jit_solution(2200735980983383203)
XLA Ops:
  16.7 5.0 collective-permute-start.2
  22.5 5.3 collective-permute-done.3
  29.1 6.4 %collective-permute-start.4 = (f32[3,1,32,128]{3,2,1,0:T(8,128)S(1)}, f32[3,1,32,128]{3,2,1,0:T(8,128)S(1)}, u32[]{:S(2)}, u32[]{:S(2)}) collective-permute-start(f32[3,1,32,128]{3,2,1,0:T(8,128)S(1)} %get-tuple-element.149), channel_id=1, source_target_pairs={{8,0},{16,8},{24,16},{32,24},{40,32},{48,40},{56,48},{64,56},{72,6... | collective-permute-start | bytes 147464 | tf_op jit(solution)/shard_map/ppermute | solution.py:27
  43.3 5.9 %collective-permute-start.8 = (f32[3,1,32,128]{3,2,1,0:T(8,128)S(1)}, f32[3,1,32,128]{3,2,1,0:T(8,128)S(1)}, u32[]{:S(2)}, u32[]{:S(2)}) collective-permute-start(f32[3,1,32,128]{3,2,1,0:T(8,128)S(1)} %get-tuple-element.144), channel_id=1, source_target_pairs={{8,0},{16,8},{24,16},{32,24},{40,32},{48,40},{56,48},{64,56},{72,6... | collective-permute-start | bytes 147464 | tf_op jit(solution)/shard_map/ppermute | solution.py:27
  56.9 6.4 %collective-permute-start.12 = (f32[3,1,32,128]{3,2,1,0:T(8,128)S(1)}, f32[3,1,32,128]{3,2,1,0:T(8,128)S(1)}, u32[]{:S(2)}, u32[]{:S(2)}) collective-permute-start(f32[3,1,32,128]{3,2,1,0:T(8,128)S(1)} %get-tuple-element.139), channel_id=1, source_target_pairs={{8,0},{16,8},{24,16},{32,24},{40,32},{48,40},{56,48},{64,56},{72,6... | collective-permute-start | bytes 147464 | tf_op jit(solution)/shard_map/ppermute | solution.py:27
  73.2 5.9 %collective-permute-start.16 = (f32[3,1,32,128]{3,2,1,0:T(8,128)S(1)}, f32[3,1,32,128]{3,2,1,0:T(8,128)S(1)}, u32[]{:S(2)}, u32[]{:S(2)}) collective-permute-start(f32[3,1,32,128]{3,2,1,0:T(8,128)S(1)} %get-tuple-element.134), channel_id=1, source_target_pairs={{8,0},{16,8},{24,16},{32,24},{40,32},{48,40},{56,48},{64,56},{72,6... | collective-permute-start | bytes 147464 | tf_op jit(solution)/shard_map/ppermute | solution.py:27
  80.7 5.4 collective-permute-start.18
  87.0 5.3 collective-permute-done.19
  92.8 5.5 %collective-permute-start.20 = (f32[3,1,32,128]{3,2,1,0:T(8,128)S(1)}, f32[3,1,32,128]{3,2,1,0:T(8,128)S(1)}, u32[]{:S(2)}, u32[]{:S(2)}) collective-permute-start(f32[3,1,32,128]{3,2,1,0:T(8,128)S(1)} %get-tuple-element.130), channel_id=1, source_target_pairs={{8,0},{16,8},{24,16},{32,24},{40,32},{48,40},{56,48},{64,56},{72,6... | collective-permute-start | bytes 147464 | tf_op jit(solution)/shard_map/ppermute | solution.py:27
  106.3 5.9 %collective-permute-start.24 = (f32[3,1,32,128]{3,2,1,0:T(8,128)S(1)}, f32[3,1,32,128]{3,2,1,0:T(8,128)S(1)}, u32[]{:S(2)}, u32[]{:S(2)}) collective-permute-start(f32[3,1,32,128]{3,2,1,0:T(8,128)S(1)} %get-tuple-element.125), channel_id=1, source_target_pairs={{8,0},{16,8},{24,16},{32,24},{40,32},{48,40},{56,48},{64,56},{72,6... | collective-permute-start | bytes 147464 | tf_op jit(solution)/shard_map/ppermute | solution.py:27
  120.0 5.9 %collective-permute-start.28 = (f32[3,1,32,128]{3,2,1,0:T(8,128)S(1)}, f32[3,1,32,128]{3,2,1,0:T(8,128)S(1)}, u32[]{:S(2)}, u32[]{:S(2)}) collective-permute-start(f32[3,1,32,128]{3,2,1,0:T(8,128)S(1)} %get-tuple-element.120), channel_id=1, source_target_pairs={{8,0},{16,8},{24,16},{32,24},{40,32},{48,40},{56,48},{64,56},{72,6... | collective-permute-start | bytes 147464 | tf_op jit(solution)/shard_map/ppermute | solution.py:27
  135.9 6.1 %collective-permute-start.32 = (f32[3,1,32,128]{3,2,1,0:T(8,128)S(1)}, f32[3,1,32,128]{3,2,1,0:T(8,128)S(1)}, u32[]{:S(2)}, u32[]{:S(2)}) collective-permute-start(f32[3,1,32,128]{3,2,1,0:T(8,128)S(1)} %get-tuple-element.115), channel_id=1, source_target_pairs={{8,0},{16,8},{24,16},{32,24},{40,32},{48,40},{56,48},{64,56},{72,6... | collective-permute-start | bytes 147464 | tf_op jit(solution)/shard_map/ppermute | solution.py:27
  143.6 5.4 collective-permute-start.34
  149.9 5.3 collective-permute-done.35
  155.7 5.5 %collective-permute-start.36 = (f32[3,1,32,128]{3,2,1,0:T(8,128)S(1)}, f32[3,1,32,128]{3,2,1,0:T(8,128)S(1)}, u32[]{:S(2)}, u32[]{:S(2)}) collective-permute-start(f32[3,1,32,128]{3,2,1,0:T(8,128)S(1)} %get-tuple-element.111), channel_id=1, source_target_pairs={{8,0},{16,8},{24,16},{32,24},{40,32},{48,40},{56,48},{64,56},{72,6... | collective-permute-start | bytes 147464 | tf_op jit(solution)/shard_map/ppermute | solution.py:27
  169.0 5.9 %collective-permute-start.40 = (f32[3,1,32,128]{3,2,1,0:T(8,128)S(1)}, f32[3,1,32,128]{3,2,1,0:T(8,128)S(1)}, u32[]{:S(2)}, u32[]{:S(2)}) collective-permute-start(f32[3,1,32,128]{3,2,1,0:T(8,128)S(1)} %get-tuple-element.106), channel_id=1, source_target_pairs={{8,0},{16,8},{24,16},{32,24},{40,32},{48,40},{56,48},{64,56},{72,6... | collective-permute-start | bytes 147464 | tf_op jit(solution)/shard_map/ppermute | solution.py:27
  182.9 5.9 %collective-permute-start.44 = (f32[3,1,32,128]{3,2,1,0:T(8,128)S(1)}, f32[3,1,32,128]{3,2,1,0:T(8,128)S(1)}, u32[]{:S(2)}, u32[]{:S(2)}) collective-permute-start(f32[3,1,32,128]{3,2,1,0:T(8,128)S(1)} %get-tuple-element.101), channel_id=1, source_target_pairs={{8,0},{16,8},{24,16},{32,24},{40,32},{48,40},{56,48},{64,56},{72,6... | collective-permute-start | bytes 147464 | tf_op jit(solution)/shard_map/ppermute | solution.py:27
  198.7 5.8 %collective-permute-start.48 = (f32[3,1,32,128]{3,2,1,0:T(8,128)S(1)}, f32[3,1,32,128]{3,2,1,0:T(8,128)S(1)}, u32[]{:S(2)}, u32[]{:S(2)}) collective-permute-start(f32[3,1,32,128]{3,2,1,0:T(8,128)S(1)} %get-tuple-element.96), channel_id=1, source_target_pairs={{8,0},{16,8},{24,16},{32,24},{40,32},{48,40},{56,48},{64,56},{72,6... | collective-permute-start | bytes 147464 | tf_op jit(solution)/shard_map/ppermute | solution.py:27
  206.0 5.4 collective-permute-start.50
  212.3 5.3 collective-permute-done.51
  218.2 5.7 %collective-permute-start.52 = (f32[3,1,32,128]{3,2,1,0:T(8,128)S(1)}, f32[3,1,32,128]{3,2,1,0:T(8,128)S(1)}, u32[]{:S(2)}, u32[]{:S(2)}) collective-permute-start(f32[3,1,32,128]{3,2,1,0:T(8,128)S(1)} %get-tuple-element.92), channel_id=1, source_target_pairs={{8,0},{16,8},{24,16},{32,24},{40,32},{48,40},{56,48},{64,56},{72,6... | collective-permute-start | bytes 147464 | tf_op jit(solution)/shard_map/ppermute | solution.py:27
  231.7 5.9 %collective-permute-start.56 = (f32[3,1,32,128]{3,2,1,0:T(8,128)S(1)}, f32[3,1,32,128]{3,2,1,0:T(8,128)S(1)}, u32[]{:S(2)}, u32[]{:S(2)}) collective-permute-start(f32[3,1,32,128]{3,2,1,0:T(8,128)S(1)} %get-tuple-element.87), channel_id=1, source_target_pairs={{8,0},{16,8},{24,16},{32,24},{40,32},{48,40},{56,48},{64,56},{72,6... | collective-permute-start | bytes 147464 | tf_op jit(solution)/shard_map/ppermute | solution.py:27
  245.4 5.9 %collective-permute-start.60 = (f32[3,1,32,128]{3,2,1,0:T(8,128)S(1)}, f32[3,1,32,128]{3,2,1,0:T(8,128)S(1)}, u32[]{:S(2)}, u32[]{:S(2)}) collective-permute-start(f32[3,1,32,128]{3,2,1,0:T(8,128)S(1)} %get-tuple-element.82), channel_id=1, source_target_pairs={{8,0},{16,8},{24,16},{32,24},{40,32},{48,40},{56,48},{64,56},{72,6... | collective-permute-start | bytes 147464 | tf_op jit(solution)/shard_map/ppermute | solution.py:27
  266.1 266.2 %all-reduce.19.cloned.1.call-done = (f32[256,6,128]{2,0,1:T(8,128)}, f32[256,6,128]{2,0,1:T(8,128)}, f32[256,6,128]{2,0,1:T(8,128)}, f32[256,6,128]{2,0,1:T(8,128)}) async-done(((f32[256,6,128]{2,0,1:T(8,128)}, f32[256,6,128]{2,0,1:T(8,128)}, f32[256,6,128]{2,0,1:T(8,128)}, f32[256,6,128]{2,0,1:T(8,128)}), (f32[256,6,128]{2,0,1:T(8,128)}, f32[256,6,128]{2,0,1:T(8,128)}, f32[256,6,128]{2,0,1:T(8,128)}, ...) | async-done | bytes 3145744 | tf_op jit(solution)/shard_map/psum | solution.py:123
  (258 shorter events, 131.5 us)
Async XLA Ops:
  7.2 525.2 %all-reduce.19.cloned.1.call-start = ((), (), s32[]{:S(2)}) async-start(), calls=%async_computation | async-start | bytes 6291456 | tf_op jit(solution)/shard_map/psum | solution.py:123
  8.1 8.6 %collective-permute-start = (f32[3,1,32,128]{3,2,1,0:T(8,128)S(1)}, f32[3,1,32,128]{3,2,1,0:T(8,128)S(1)}, u32[]{:S(2)}, u32[]{:S(2)}) collective-permute-start(f32[3,1,32,128]{3,2,1,0:T(8,128)S(1)} %get-tuple-element.153), channel_id=1, source_target_pairs={{8,0},{16,8},{24,16},{32,24},{40,32},{48,40},{56,48},{64,56},{72,6... | collective-permute-start | bytes 147464 | tf_op jit(solution)/shard_map/ppermute | solution.py:27
  29.0 7.1 %collective-permute-start.5 = (f32[3,1,32,128]{3,2,1,0:T(8,128)S(1)}, f32[3,1,32,128]{3,2,1,0:T(8,128)S(1)}, u32[]{:S(2)}, u32[]{:S(2)}) collective-permute-start(f32[3,1,32,128]{3,2,1,0:T(8,128)S(1)} %get-tuple-element.148), channel_id=1, source_target_pairs={{0,8},{8,16},{16,24},{24,32},{32,40},{40,48},{48,56},{56,64},{64,7... | collective-permute-start | bytes 147464 | tf_op jit(solution)/shard_map/ppermute | solution.py:25
  29.1 7.3 %collective-permute-start.4 = (f32[3,1,32,128]{3,2,1,0:T(8,128)S(1)}, f32[3,1,32,128]{3,2,1,0:T(8,128)S(1)}, u32[]{:S(2)}, u32[]{:S(2)}) collective-permute-start(f32[3,1,32,128]{3,2,1,0:T(8,128)S(1)} %get-tuple-element.149), channel_id=1, source_target_pairs={{8,0},{16,8},{24,16},{32,24},{40,32},{48,40},{56,48},{64,56},{72,6... | collective-permute-start | bytes 147464 | tf_op jit(solution)/shard_map/ppermute | solution.py:27
  43.3 6.8 %collective-permute-start.8 = (f32[3,1,32,128]{3,2,1,0:T(8,128)S(1)}, f32[3,1,32,128]{3,2,1,0:T(8,128)S(1)}, u32[]{:S(2)}, u32[]{:S(2)}) collective-permute-start(f32[3,1,32,128]{3,2,1,0:T(8,128)S(1)} %get-tuple-element.144), channel_id=1, source_target_pairs={{8,0},{16,8},{24,16},{32,24},{40,32},{48,40},{56,48},{64,56},{72,6... | collective-permute-start | bytes 147464 | tf_op jit(solution)/shard_map/ppermute | solution.py:27
  56.8 6.8 %collective-permute-start.13 = (f32[3,1,32,128]{3,2,1,0:T(8,128)S(1)}, f32[3,1,32,128]{3,2,1,0:T(8,128)S(1)}, u32[]{:S(2)}, u32[]{:S(2)}) collective-permute-start(f32[3,1,32,128]{3,2,1,0:T(8,128)S(1)} %get-tuple-element.138), channel_id=1, source_target_pairs={{0,8},{8,16},{16,24},{24,32},{32,40},{40,48},{48,56},{56,64},{64,7... | collective-permute-start | bytes 147464 | tf_op jit(solution)/shard_map/ppermute | solution.py:25
  56.9 7.3 %collective-permute-start.12 = (f32[3,1,32,128]{3,2,1,0:T(8,128)S(1)}, f32[3,1,32,128]{3,2,1,0:T(8,128)S(1)}, u32[]{:S(2)}, u32[]{:S(2)}) collective-permute-start(f32[3,1,32,128]{3,2,1,0:T(8,128)S(1)} %get-tuple-element.139), channel_id=1, source_target_pairs={{8,0},{16,8},{24,16},{32,24},{40,32},{48,40},{56,48},{64,56},{72,6... | collective-permute-start | bytes 147464 | tf_op jit(solution)/shard_map/ppermute | solution.py:27
  73.1 7.5 %collective-permute-start.17 = (f32[3,1,32,128]{3,2,1,0:T(8,128)S(1)}, f32[3,1,32,128]{3,2,1,0:T(8,128)S(1)}, u32[]{:S(2)}, u32[]{:S(2)}) collective-permute-start(f32[3,1,32,128]{3,2,1,0:T(8,128)S(1)} %get-tuple-element.133), channel_id=1, source_target_pairs={{0,8},{8,16},{16,24},{24,32},{32,40},{40,48},{48,56},{56,64},{64,7... | collective-permute-start | bytes 147464 | tf_op jit(solution)/shard_map/ppermute | solution.py:25
  73.2 7.5 %collective-permute-start.16 = (f32[3,1,32,128]{3,2,1,0:T(8,128)S(1)}, f32[3,1,32,128]{3,2,1,0:T(8,128)S(1)}, u32[]{:S(2)}, u32[]{:S(2)}) collective-permute-start(f32[3,1,32,128]{3,2,1,0:T(8,128)S(1)} %get-tuple-element.134), channel_id=1, source_target_pairs={{8,0},{16,8},{24,16},{32,24},{40,32},{48,40},{56,48},{64,56},{72,6... | collective-permute-start | bytes 147464 | tf_op jit(solution)/shard_map/ppermute | solution.py:27
  106.3 6.8 %collective-permute-start.24 = (f32[3,1,32,128]{3,2,1,0:T(8,128)S(1)}, f32[3,1,32,128]{3,2,1,0:T(8,128)S(1)}, u32[]{:S(2)}, u32[]{:S(2)}) collective-permute-start(f32[3,1,32,128]{3,2,1,0:T(8,128)S(1)} %get-tuple-element.125), channel_id=1, source_target_pairs={{8,0},{16,8},{24,16},{32,24},{40,32},{48,40},{56,48},{64,56},{72,6... | collective-permute-start | bytes 147464 | tf_op jit(solution)/shard_map/ppermute | solution.py:27
  119.9 7.0 %collective-permute-start.29 = (f32[3,1,32,128]{3,2,1,0:T(8,128)S(1)}, f32[3,1,32,128]{3,2,1,0:T(8,128)S(1)}, u32[]{:S(2)}, u32[]{:S(2)}) collective-permute-start(f32[3,1,32,128]{3,2,1,0:T(8,128)S(1)} %get-tuple-element.119), channel_id=1, source_target_pairs={{0,8},{8,16},{16,24},{24,32},{32,40},{40,48},{48,56},{56,64},{64,7... | collective-permute-start | bytes 147464 | tf_op jit(solution)/shard_map/ppermute | solution.py:25
  120.0 6.9 %collective-permute-start.28 = (f32[3,1,32,128]{3,2,1,0:T(8,128)S(1)}, f32[3,1,32,128]{3,2,1,0:T(8,128)S(1)}, u32[]{:S(2)}, u32[]{:S(2)}) collective-permute-start(f32[3,1,32,128]{3,2,1,0:T(8,128)S(1)} %get-tuple-element.120), channel_id=1, source_target_pairs={{8,0},{16,8},{24,16},{32,24},{40,32},{48,40},{56,48},{64,56},{72,6... | collective-permute-start | bytes 147464 | tf_op jit(solution)/shard_map/ppermute | solution.py:27
  135.8 7.7 %collective-permute-start.33 = (f32[3,1,32,128]{3,2,1,0:T(8,128)S(1)}, f32[3,1,32,128]{3,2,1,0:T(8,128)S(1)}, u32[]{:S(2)}, u32[]{:S(2)}) collective-permute-start(f32[3,1,32,128]{3,2,1,0:T(8,128)S(1)} %get-tuple-element.114), channel_id=1, source_target_pairs={{0,8},{8,16},{16,24},{24,32},{32,40},{40,48},{48,56},{56,64},{64,7... | collective-permute-start | bytes 147464 | tf_op jit(solution)/shard_map/ppermute | solution.py:25
  135.9 7.7 %collective-permute-start.32 = (f32[3,1,32,128]{3,2,1,0:T(8,128)S(1)}, f32[3,1,32,128]{3,2,1,0:T(8,128)S(1)}, u32[]{:S(2)}, u32[]{:S(2)}) collective-permute-start(f32[3,1,32,128]{3,2,1,0:T(8,128)S(1)} %get-tuple-element.115), channel_id=1, source_target_pairs={{8,0},{16,8},{24,16},{32,24},{40,32},{48,40},{56,48},{64,56},{72,6... | collective-permute-start | bytes 147464 | tf_op jit(solution)/shard_map/ppermute | solution.py:27
  168.9 6.7 %collective-permute-start.41 = (f32[3,1,32,128]{3,2,1,0:T(8,128)S(1)}, f32[3,1,32,128]{3,2,1,0:T(8,128)S(1)}, u32[]{:S(2)}, u32[]{:S(2)}) collective-permute-start(f32[3,1,32,128]{3,2,1,0:T(8,128)S(1)} %get-tuple-element.105), channel_id=1, source_target_pairs={{0,8},{8,16},{16,24},{24,32},{32,40},{40,48},{48,56},{56,64},{64,7... | collective-permute-start | bytes 147464 | tf_op jit(solution)/shard_map/ppermute | solution.py:25
  169.0 6.8 %collective-permute-start.40 = (f32[3,1,32,128]{3,2,1,0:T(8,128)S(1)}, f32[3,1,32,128]{3,2,1,0:T(8,128)S(1)}, u32[]{:S(2)}, u32[]{:S(2)}) collective-permute-start(f32[3,1,32,128]{3,2,1,0:T(8,128)S(1)} %get-tuple-element.106), channel_id=1, source_target_pairs={{8,0},{16,8},{24,16},{32,24},{40,32},{48,40},{56,48},{64,56},{72,6... | collective-permute-start | bytes 147464 | tf_op jit(solution)/shard_map/ppermute | solution.py:27
  182.8 7.0 %collective-permute-start.45 = (f32[3,1,32,128]{3,2,1,0:T(8,128)S(1)}, f32[3,1,32,128]{3,2,1,0:T(8,128)S(1)}, u32[]{:S(2)}, u32[]{:S(2)}) collective-permute-start(f32[3,1,32,128]{3,2,1,0:T(8,128)S(1)} %get-tuple-element.100), channel_id=1, source_target_pairs={{0,8},{8,16},{16,24},{24,32},{32,40},{40,48},{48,56},{56,64},{64,7... | collective-permute-start | bytes 147464 | tf_op jit(solution)/shard_map/ppermute | solution.py:25
  182.9 6.9 %collective-permute-start.44 = (f32[3,1,32,128]{3,2,1,0:T(8,128)S(1)}, f32[3,1,32,128]{3,2,1,0:T(8,128)S(1)}, u32[]{:S(2)}, u32[]{:S(2)}) collective-permute-start(f32[3,1,32,128]{3,2,1,0:T(8,128)S(1)} %get-tuple-element.101), channel_id=1, source_target_pairs={{8,0},{16,8},{24,16},{32,24},{40,32},{48,40},{56,48},{64,56},{72,6... | collective-permute-start | bytes 147464 | tf_op jit(solution)/shard_map/ppermute | solution.py:27
  198.6 7.4 %collective-permute-start.49 = (f32[3,1,32,128]{3,2,1,0:T(8,128)S(1)}, f32[3,1,32,128]{3,2,1,0:T(8,128)S(1)}, u32[]{:S(2)}, u32[]{:S(2)}) collective-permute-start(f32[3,1,32,128]{3,2,1,0:T(8,128)S(1)} %get-tuple-element.95), channel_id=1, source_target_pairs={{0,8},{8,16},{16,24},{24,32},{32,40},{40,48},{48,56},{56,64},{64,7... | collective-permute-start | bytes 147464 | tf_op jit(solution)/shard_map/ppermute | solution.py:25
  198.7 7.3 %collective-permute-start.48 = (f32[3,1,32,128]{3,2,1,0:T(8,128)S(1)}, f32[3,1,32,128]{3,2,1,0:T(8,128)S(1)}, u32[]{:S(2)}, u32[]{:S(2)}) collective-permute-start(f32[3,1,32,128]{3,2,1,0:T(8,128)S(1)} %get-tuple-element.96), channel_id=1, source_target_pairs={{8,0},{16,8},{24,16},{32,24},{40,32},{48,40},{56,48},{64,56},{72,6... | collective-permute-start | bytes 147464 | tf_op jit(solution)/shard_map/ppermute | solution.py:27
  231.6 6.8 %collective-permute-start.57 = (f32[3,1,32,128]{3,2,1,0:T(8,128)S(1)}, f32[3,1,32,128]{3,2,1,0:T(8,128)S(1)}, u32[]{:S(2)}, u32[]{:S(2)}) collective-permute-start(f32[3,1,32,128]{3,2,1,0:T(8,128)S(1)} %get-tuple-element.86), channel_id=1, source_target_pairs={{0,8},{8,16},{16,24},{24,32},{32,40},{40,48},{48,56},{56,64},{64,7... | collective-permute-start | bytes 147464 | tf_op jit(solution)/shard_map/ppermute | solution.py:25
  231.7 6.8 %collective-permute-start.56 = (f32[3,1,32,128]{3,2,1,0:T(8,128)S(1)}, f32[3,1,32,128]{3,2,1,0:T(8,128)S(1)}, u32[]{:S(2)}, u32[]{:S(2)}) collective-permute-start(f32[3,1,32,128]{3,2,1,0:T(8,128)S(1)} %get-tuple-element.87), channel_id=1, source_target_pairs={{8,0},{16,8},{24,16},{32,24},{40,32},{48,40},{56,48},{64,56},{72,6... | collective-permute-start | bytes 147464 | tf_op jit(solution)/shard_map/ppermute | solution.py:27
  245.3 7.0 %collective-permute-start.61 = (f32[3,1,32,128]{3,2,1,0:T(8,128)S(1)}, f32[3,1,32,128]{3,2,1,0:T(8,128)S(1)}, u32[]{:S(2)}, u32[]{:S(2)}) collective-permute-start(f32[3,1,32,128]{3,2,1,0:T(8,128)S(1)} %get-tuple-element.81), channel_id=1, source_target_pairs={{0,8},{8,16},{16,24},{24,32},{32,40},{40,48},{48,56},{56,64},{64,7... | collective-permute-start | bytes 147464 | tf_op jit(solution)/shard_map/ppermute | solution.py:25
  245.4 6.9 %collective-permute-start.60 = (f32[3,1,32,128]{3,2,1,0:T(8,128)S(1)}, f32[3,1,32,128]{3,2,1,0:T(8,128)S(1)}, u32[]{:S(2)}, u32[]{:S(2)}) collective-permute-start(f32[3,1,32,128]{3,2,1,0:T(8,128)S(1)} %get-tuple-element.82), channel_id=1, source_target_pairs={{8,0},{16,8},{24,16},{32,24},{40,32},{48,40},{56,48},{64,56},{72,6... | collective-permute-start | bytes 147464 | tf_op jit(solution)/shard_map/ppermute | solution.py:27
  (51 other events, 263.1 us)
Sparse Core Ops, SparseCore 0:
  265.3 266.9 all-reduce.18
where the time goes:
time: 556 us; the launch traced here: 547 us
  waiting for transfers between devices  329 us (59%)
  starting transfers between devices  160 us (29%)
  matrix products  20.1 us (4%)
  between operations  18 us (3%)
  other arithmetic  11.2 us (2%)
  local copies, waits for them, and re-layouts  8.84 us (2%)
    psum x1, waiting for transfers between devices, on_device(): summed = lax.psum(coefs, ('gx', 'gz'))  266 us
    ppermute x32, starting transfers between devices, padded_2(): lax.ppermute(head, axis, [((i + 1) % count, i) for i in range(count)])  131 us
    ppermute x32, waiting for transfers between devices, padded_2(): lax.ppermute(tail, axis, [(i, (i + 1) % count) for i in range(count)])  48.5 us
    ppermute x32, starting transfers between devices, padded_2(): lax.ppermute(tail, axis, [(i, (i + 1) % count) for i in range(count)])  29.3 us
    ppermute x32, waiting for transfers between devices, padded_2(): lax.ppermute(head, axis, [((i + 1) % count, i) for i in range(count)])  14.1 us
  transfers between devices with their start and end apart: 65, of which 42 were waited for; matrix products, arithmetic and copies ran while one was open for 2% of the time, Pallas kernels for 0%

commit v1 on v0

v1 whole, which is shorter than its diff:
```python
import functools
import math

import numpy as np

import jax
import jax.numpy as jnp
from jax import lax
from jax.experimental import pallas as pl
from jax.experimental.pallas import tpu as pltpu
from jax.sharding import PartitionSpec as P

KX = 16
KZ = 16
STEP = 0.05
BASE_VISCOSITY = 0.02
DRIVE = 0.5
DISCOUNT = 0.97
HALO = 4
MESH = pl.DeviceIdType.MESH
HIGH = lax.Precision.HIGHEST


def z_table(peers, cells_x, cells_z, total_x, total_z):
    own = KZ // peers
    factor = 1.0 / math.sqrt(total_x * total_z)
    spots = np.arange(peers)[:, None] * cells_z + np.arange(cells_z)[None, :]
    turns = (np.arange(KZ)[None, :, None] * spots[:, None, :]) % total_z
    angle = turns * (2.0 * math.pi / total_z)
    waves = np.stack([np.cos(angle), -np.sin(angle)], axis=2) * factor
    eye = np.eye(cells_x)
    table = np.einsum("gkrz,ab->gkraBz".replace("B", "b"), waves, eye)
    rows = peers * own * 2 * cells_x
    return table.reshape(peers, rows, cells_x * cells_z).astype(np.float32)


def x_table(devices, peers, cells_x, total_x):
    own = KZ // peers
    spots = np.arange(devices)[:, None] * cells_x + np.arange(cells_x)[None, :]
    turns = (np.arange(KX)[None, :, None] * spots[:, None, :]) % total_x
    angle = turns * (2.0 * math.pi / total_x)
    c, s = np.cos(angle), np.sin(angle)
    spin = np.stack([np.stack([c, s], 2), np.stack([-s, c], 2)], 1)
    eye = np.eye(own)
    table = np.einsum("gqkrx,ab->gqkabrx", spin, eye)
    table = table.reshape(devices, 2 * KX * own, 1, own * 2 * cells_x)
    table = np.broadcast_to(table, (devices, 2 * KX * own, peers, own * 2 * cells_x))
    return table.reshape(devices, 2 * KX * own, peers * own * 2 * cells_x).astype(np.float32)


def kernel(
    ngx,
    ngz,
    vel,
    eddy,
    target,
    mean,
    past,
    boot,
    t1_hbm,
    t2_hbm,
    out_vel,
    out_ret,
    field,
    w2,
    w3,
    w4,
    nu,
    pack,
    zc,
    t1,
    t2,
    q_buf,
    r_buf,
    p_buf,
    s_buf,
    loc,
    term,
    a_buf,
    b_tile,
    b_buf,
    local_sem,
    halo_send,
    halo_recv,
    gz_send,
    gz_recv,
    gx_send,
    gx_recv,
    ar_send,
    ar_recv,
):
    gx = lax.axis_index("gx")
    gz = lax.axis_index("gz")
    steps = eddy.shape[0]
    nx = vel.shape[1]
    nz = vel.shape[2]
    ny = vel.shape[3]
    span = nz + 2 * HALO
    rows = (nx + 2 * HALO + 1) * span
    past_steps = past.shape[0]

    def xpeer(d):
        return lax.rem(gx + d + ngx, ngx)

    def zpeer(d):
        return lax.rem(gz + d + ngz, ngz)

    load_vel = pltpu.make_async_copy(
        vel, field.at[0, 0:3, pl.ds(HALO + 1, nx), 0:nz, :], local_sem.at[0]
    )
    load_t1 = pltpu.make_async_copy(t1_hbm.at[gz], t1, local_sem.at[1])
    load_t2 = pltpu.make_async_copy(t2_hbm.at[gx], t2, local_sem.at[2])
    load_vel.start()
    load_t1.start()
    load_t2.start()

    barrier = pltpu.get_barrier_semaphore()

    def greet_x(d, carry):
        pl.semaphore_signal(barrier, inc=1, device_id=(xpeer(d), gz), device_id_type=MESH)
        return carry

    def greet_z(d, carry):
        pl.semaphore_signal(barrier, inc=1, device_id=(gx, zpeer(d)), device_id_type=MESH)
        return carry

    lax.fori_loop(1, ngx, greet_x, 0)
    lax.fori_loop(1, ngz, greet_z, 0)
    for dx in (-1, 1):
        for dz in (-1, 1):
            pl.semaphore_signal(
                barrier, inc=1, device_id=(xpeer(dx), zpeer(dz)), device_id_type=MESH
            )

    eye = (
        lax.broadcasted_iota(jnp.int32, (steps, ny), 0)
        == lax.broadcasted_iota(jnp.int32, (steps, ny), 1)
    ).astype(jnp.float32)
    for x in range(nx):
        field[0, 3, HALO + 1 + x, 0:nz, :] = lax.dot_general(
            eddy[:, x, :],
            eye,
            (((0,), (0,)), ((), ())),
            precision=HIGH,
            preferred_element_type=jnp.float32,
        )

    def halo_copies(s, comps):
        copies = []
        first = HALO + 1
        for index, (dx, src, dst) in enumerate(
            ((1, first + nx - HALO, 1), (-1, first, first + nx))
        ):
            copies.append(
                pltpu.make_async_remote_copy(
                    src_ref=field.at[s, 0:comps, pl.ds(src, HALO), 0:nz, :],
                    dst_ref=field.at[s, 0:comps, pl.ds(dst, HALO), 0:nz, :],
                    send_sem=halo_send.at[s, index],
                    recv_sem=halo_recv.at[s, index],
                    device_id=(xpeer(dx), gz),
                    device_id_type=MESH,
                )
            )
        for side, dz in ((0, 1), (1, -1)):
            for index, (dx, src, dst, count) in enumerate(
                ((0, 0, HALO, nx), (1, nx - HALO, 0, HALO), (-1, 0, HALO + nx, HALO))
            ):
                copies.append(
                    pltpu.make_async_remote_copy(
                        src_ref=pack.at[s, side, 0:comps, pl.ds(src, count), :, :],
                        dst_ref=zc.at[s, side, 0:comps, pl.ds(dst, count), :, :],
                        send_sem=halo_send.at[s, 2 + 3 * side + index],
                        recv_sem=halo_recv.at[s, 2 + 3 * side + index],
                        device_id=(xpeer(dx), zpeer(dz)),
                        device_id_type=MESH,
                    )
                )
        return copies

    def start_halo(s, comps):
        first = HALO + 1
        for c in range(comps):
            pack[s, 0, c] = field[s, c, pl.ds(first, nx), nz - HALO : nz, :]
            pack[s, 1, c] = field[s, c, pl.ds(first, nx), 0:HALO, :]
        for copy in halo_copies(s, comps):
            copy.start()

    def wait_halo(s, comps):
        copies = halo_copies(s, comps)
        for copy in copies:
            copy.wait_recv()
        total = nx + 2 * HALO
        for c in range(comps):
            field[s, c, 0:total, nz + HALO : span, :] = zc[s, 0, c]
            field[s, c, 1 : total + 1, nz : nz + HALO, :] = zc[s, 1, c]
        for copy in copies:
            copy.wait_send()

    lane = lax.broadcasted_iota(jnp.int32, (8, ny), 1)
    mask_plus = (lane < ny - 1).astype(jnp.float32)
    mask_minus = (lane > 0).astype(jnp.float32)
    rows_y = lane[0:1].astype(jnp.float32) + 0.5
    wall = jnp.minimum(rows_y, ny - rows_y) / (ny / 2.0)

    def tendency(src, nu_s, r):
        around = [src.at[c, pl.ds(pl.multiple_of(r - 8, 8), 24), :] for c in range(3)]
        mid = [src[c, pl.ds(pl.multiple_of(r, 8), 8), :] for c in range(3)]
        visc = nu_s[pl.ds(pl.multiple_of(r, 8), 8), :]
        hu, hw, hv = mid[0] * 0.5, mid[1] * 0.5, mid[2] * 0.5
        x_plus, x_minus = visc - hu, visc + hu
        z_plus, z_minus = visc - hw, visc + hw
        y_plus, y_minus = (visc - hv) * mask_plus, (visc + hv) * mask_minus
        center = visc * -6.0
        out = []
        for c in range(3):
            value = center * mid[c]
            value += x_plus * src[c, pl.ds(pl.multiple_of(r + span, 8), 8), :]
            value += x_minus * src[c, pl.ds(pl.multiple_of(r - span, 8), 8), :]
            value += z_plus * around[c][9:17, :]
            value += z_minus * around[c][7:15, :]
            value += y_plus * pltpu.roll(mid[c], ny - 1, 1)
            value += y_minus * pltpu.roll(mid[c], 1, 1)
            if c == 0:
                value += DRIVE
            out.append(value)
        return mid, out

    def stages(s):
        v0 = field.at[s].reshape(4, rows, ny)
        v1 = field.at[s + 1].reshape(4, rows, ny)
        nu_s = nu.at[s].reshape(rows, ny)
        for k, (src, dst, scale) in enumerate(
            ((v0, w2, 0.5 * STEP), (w2, w3, 0.5 * STEP), (w3, w4, STEP)), 1
        ):

            def one(r, src=src, dst=dst, scale=scale):
                mid, out = tendency(src, nu_s, r)
                for c in range(3):
                    base = v0[c, pl.ds(pl.multiple_of(r, 8), 8), :]
                    dst[c, pl.ds(pl.multiple_of(r, 8), 8), :] = base + scale * out[c]

            def line(i, carry, k=k, one=one):
                start = k * span + nz + i * span
                for t in range(span // 8):
                    one(start + 8 * t)
                return carry

            total = nx + 2 * HALO
            lax.fori_loop(0, total - 2 * k, line, 0)
            one((total + 1 - k) * span - 8)

        def last(i, carry):
            start = (HALO + 1 + i) * span
            for t in range(nz // 8):
                r = start + 8 * t
                here = pl.ds(pl.multiple_of(r, 8), 8)
                mid, out = tendency(w4, nu_s, r)
                for c in range(3):
                    mean_part = (w2[c, here, :] + mid[c] - v0[c, here, :]) + 2.0 * w3[c, here, :]
                    v1[c, here, :] = mean_part * (1.0 / 3.0) + (STEP / 6.0) * out[c]
            return carry

        lax.fori_loop(0, nx, last, 0)

    def interior(s, c):
        return field[s, c, pl.ds(HALO + 1, nx), 0:nz, :]

    def start_gz(s):
        cells = nx * nz
        for c in range(3):
            value = interior(s + 1, c).reshape(cells, ny)
            part = jnp.dot(t1[...], value, precision=HIGH, preferred_element_type=jnp.float32)
            q_buf[s, :, c] = part.reshape(ngz, part.shape[0] // ngz, ny)

        def send(d, carry):
            pltpu.make_async_remote_copy(
                src_ref=q_buf.at[s, zpeer(d)],
                dst_ref=r_buf.at[s, d - 1],
                send_sem=gz_send.at[s],
                recv_sem=gz_recv.at[s],
                device_id=(gx, zpeer(d)),
                device_id_type=MESH,
            ).start()
            return carry

        lax.fori_loop(1, ngz, send, 0)
        r_buf[s, ngz - 1] = q_buf[s, gz]

    def wait_bytes(ref, sem):
        pltpu.make_async_copy(ref, ref, sem).wait()

    def start_gx(s):
        wait_bytes(r_buf.at[s, 0 : ngz - 1], gz_recv.at[s])
        p_flat = p_buf.at[s].reshape(ngx * 8, ny)
        for c in range(3):
            value = r_buf[s, :, c].reshape(t2.shape[1], ny)
            part = jnp.dot(t2[...], value, precision=HIGH, preferred_element_type=jnp.float32)
            for q in range(2):
                p_flat[pl.ds(2 * c + q, ngx, stride=8), :] = part[q * ngx : (q + 1) * ngx]
        for q in (6, 7):
            p_flat[pl.ds(q, ngx, stride=8), :] = jnp.zeros((ngx, ny), jnp.float32)

        def send(d, carry):
            pltpu.make_async_remote_copy(
                src_ref=p_buf.at[s, xpeer(d)],
                dst_ref=s_buf.at[s, d - 1],
                send_sem=gx_send.at[s],
                recv_sem=gx_recv.at[s],
                device_id=(xpeer(d), gz),
                device_id_type=MESH,
            ).start()
            return carry

        lax.fori_loop(1, ngx, send, 0)
        s_buf[s, ngx - 1] = p_buf[s, gx]

    def finish_gx(s):
        wait_bytes(s_buf.at[s, 0 : ngx - 1], gx_recv.at[s])
        coefs = jnp.sum(s_buf[s], axis=0)
        energy = jnp.sum(coefs * coefs) * (1.0 / ny)
        own = KZ // ngz
        wave = (gx // own) * KZ + gz * own + lax.rem(gx, own)
        energy = jnp.full((1, ny), energy, jnp.float32)
        goal = jnp.full((1, ny), target[wave], jnp.float32)
        ratio = (energy - goal) / (energy + goal)
        term[pl.ds(s, 1), :] = ratio * ratio

    def local_reward(s):
        offset = interior(s + 1, 0) - mean[...].reshape(1, 1, ny)
        square = offset * offset
        wide = jnp.concatenate([square[x] for x in range(nx)], axis=1)
        pick = (
            lax.broadcasted_iota(jnp.int32, (nx, nx * ny), 1) // ny
            == lax.broadcasted_iota(jnp.int32, (nx, nx * ny), 0)
        ).astype(jnp.float32)
        total = lax.dot_general(
            pick,
            wide,
            (((1,), (1,)), ((), ())),
            precision=HIGH,
            preferred_element_type=jnp.float32,
        )
        loc[s] = total * (-1.0 / ny)

    term[...] = jnp.zeros_like(term)
    load_vel.wait()
    pl.semaphore_wait(barrier, ngx + ngz + 2)
    start_halo(0, 4)
    load_t1.wait()
    load_t2.wait()
    wait_halo(0, 4)

    def viscosity(i, carry):
        each = field[0, 3, i]
        for s in range(steps):
            nu[s, i] = BASE_VISCOSITY + each[:, s : s + 1] * wall
        return carry

    lax.fori_loop(0, nx + 2 * HALO + 1, viscosity, 0)

    def body(s, carry):
        stages(s)

        @pl.when(s < steps - 1)
        def _():
            start_halo(s + 1, 3)

        start_gz(s)
        local_reward(s)

        @pl.when(s >= 1)
        def _():
            start_gx(s - 1)

        @pl.when(s >= 2)
        def _():
            finish_gx(s - 2)

        @pl.when(s < steps - 1)
        def _():
            wait_halo(s + 1, 3)

        return carry

    lax.fori_loop(0, steps, body, 0)

    store_vel = pltpu.make_async_copy(
        field.at[steps, 0:3, pl.ds(HALO + 1, nx), 0:nz, :], out_vel, local_sem.at[0]
    )
    store_vel.start()
    finish_gx(steps - 2)
    start_gx(steps - 1)

    plain = [None] * (past_steps + steps)
    running = boot[...]
    for t in range(past_steps + steps - 1, -1, -1):
        reward = past[t] if t < past_steps else loc[t - past_steps]
        running = reward + DISCOUNT * running
        plain[t] = running

    finish_gx(steps - 1)

    def send_x(d, carry):
        pltpu.make_async_remote_copy(
            src_ref=term,
            dst_ref=a_buf.at[d - 1],
            send_sem=ar_send.at[0],
            recv_sem=ar_recv.at[0],
            device_id=(xpeer(d), gz),
            device_id_type=MESH,
        ).start()
        return carry

    lax.fori_loop(1, ngx, send_x, 0)
    wait_bytes(a_buf, ar_recv.at[0])
    b_tile[...] = term[...] + jnp.sum(a_buf[...], axis=0)

    def send_z(d, carry):
        pltpu.make_async_remote_copy(
            src_ref=b_tile,
            dst_ref=b_buf.at[d - 1],
            send_sem=ar_send.at[1],
            recv_sem=ar_recv.at[1],
            device_id=(gx, zpeer(d)),
            device_id_type=MESH,
        ).start()
        return carry

    lax.fori_loop(1, ngz, send_z, 0)
    wait_bytes(b_buf, ar_recv.at[1])
    spectrum = (b_tile[...] + jnp.sum(b_buf[...], axis=0)) * (-1.0 / KX)

    extra = None
    for t in range(past_steps + steps - 1, -1, -1):
        if extra is not None:
            extra = extra * DISCOUNT
        if t >= past_steps:
            new = spectrum[t - past_steps : t - past_steps + 1, 0:nz]
            extra = new if extra is None else extra + new
        out_ret[t] = plain[t] + extra

    def drain(s, carry):
        wait_bytes(r_buf.at[s, 0 : ngz - 1], gz_send.at[s])
        wait_bytes(s_buf.at[s, 0 : ngx - 1], gx_send.at[s])
        return carry

    lax.fori_loop(0, steps, drain, 0)
    wait_bytes(a_buf, ar_send.at[0])
    wait_bytes(b_buf, ar_send.at[1])
    store_vel.wait()


def on_device(
    ngx, ngz, velocity, eddy_viscosity, target_spectrum, mean_profile, past_rewards, bootstrap_values
):
    nx, nz, ny = velocity.shape[1:]
    steps = eddy_viscosity.shape[0]
    horizon = past_rewards.shape[0] + steps
    t1 = z_table(ngz, nx, nz, nx * ngx, nz * ngz)
    t2 = x_table(ngx, ngz, nx, nx * ngx)
    span = nz + 2 * HALO
    lines = nx + 2 * HALO + 1
    f32 = jnp.float32
    vmem = pl.BlockSpec(memory_space=pltpu.VMEM)
    hbm = pl.BlockSpec(memory_space=pl.ANY)
    smem = pl.BlockSpec(memory_space=pltpu.SMEM)
    dma = pltpu.SemaphoreType.DMA
    return pl.pallas_call(
        functools.partial(kernel, ngx, ngz),
        out_shape=(
            jax.ShapeDtypeStruct(velocity.shape, f32),
            jax.ShapeDtypeStruct((horizon, nx, nz), f32),
        ),
        in_specs=[hbm, vmem, smem, vmem, vmem, vmem, hbm, hbm],
        out_specs=(hbm, vmem),
        scratch_shapes=[
            pltpu.VMEM((steps + 1, 4, lines, span, ny), f32),
            pltpu.VMEM((3, lines * span, ny), f32),
            pltpu.VMEM((3, lines * span, ny), f32),
            pltpu.VMEM((3, lines * span, ny), f32),
            pltpu.VMEM((steps, lines, span, ny), f32),
            pltpu.VMEM((steps, 2, 4, nx, HALO, ny), f32),
            pltpu.VMEM((steps, 2, 4, nx + 2 * HALO, HALO, ny), f32),
            pltpu.VMEM(t1.shape[1:], f32),
            pltpu.VMEM(t2.shape[1:], f32),
            pltpu.VMEM((steps, ngz, 3, t1.shape[1] // ngz, ny), f32),
            pltpu.VMEM((steps, ngz, 3, t1.shape[1] // ngz, ny), f32),
            pltpu.VMEM((steps, ngx, 8, ny), f32),
            pltpu.VMEM((steps, ngx, 8, ny), f32),
            pltpu.VMEM((steps, nx, nz), f32),
            pltpu.VMEM((8, ny), f32),
            pltpu.VMEM((ngx - 1, 8, ny), f32),
            pltpu.VMEM((8, ny), f32),
            pltpu.VMEM((ngz - 1, 8, ny), f32),
            dma((3,)),
            dma((steps, 8)),
            dma((steps, 8)),
            dma((steps,)),
            dma((steps,)),
            dma((steps,)),
            dma((steps,)),
            dma((2,)),
            dma((2,)),
        ],
        compiler_params=pltpu.CompilerParams(
            collective_id=0, has_side_effects=True, vmem_limit_bytes=48 * 1024 * 1024
        ),
        name="rollout",
    )(
        velocity,
        eddy_viscosity,
        target_spectrum,
        mean_profile.reshape(1, ny),
        past_rewards,
        bootstrap_values,
        jnp.asarray(t1),
        jnp.asarray(t2),
    )


def solution(mesh):
    placed = (
        P(None, "gx", "gz", None),
        P(None, "gx", "gz"),
        P(),
        P(),
        P(None, "gx", "gz"),
        P("gx", "gz"),
    )
    return jax.shard_map(
        functools.partial(on_device, mesh.shape["gx"], mesh.shape["gz"]),
        mesh=mesh,
        in_specs=placed,
        out_specs=(P(None, "gx", "gz", None), P(None, "gx", "gz")),
        check_vma=False,
    )
```

time: 556 us -> 110 us (0.20); the launches traced: 547 us -> 110 us
  waiting for transfers between devices: 329 us -> 0 us
  starting transfers between devices: 160 us -> 0 us
  Pallas kernels: 0 us -> 100 us
  matrix products: 20.1 us -> 0 us
  between operations: 18 us -> 0.66 us
  other arithmetic: 11.2 us -> 0 us
    psum x1 -> x0, waiting for transfers between devices: 266 us -> none  [on_device(): summed = lax.psum(coefs, ('gx', 'gz'))]
    ppermute x64 -> x0, starting transfers between devices: 160 us -> none  [the longest x32 131 us: padded_2(): lax.ppermute(head, axis, [((i + 1) % count, i) for i in range(count)])]
    pallas_call x0 -> x1, Pallas kernels: none -> 100 us  [on_device(): pl.pallas_call(functools.partial(kernel, ngx, ngz), out_shape=(jax.ShapeD...]
    ppermute x64 -> x0, waiting for transfers between devices: 62.6 us -> none  [the longest x32 48.5 us: padded_2(): lax.ppermute(tail, axis, [(i, (i + 1) % count) for i in range(count)])]
    dot_general x24 -> x0, matrix products: 20.1 us -> none  [the longest x4 4.08 us: mode_sums(): part_c = jnp.einsum('kx,cxzy->kczy', cos_x, field, precision=high)]
    add x20 -> x0, other arithmetic: 7.2 us -> none  [the longest x4 1.91 us: advance(): field + step_length / 6.0 * (first + 2.0 * second + 2.0 * third + fourth)]
    unnamed x29 -> x18, local copies, waits for them, and re-layouts: 3.24 us -> 9.08 us
  transfers between devices with their start and end apart: 65 -> 0, of which waited for: 42 -> 0; matrix products, arithmetic and copies ran while one was open for 2% -> 0% of each run, Pallas kernels for 0% -> 0%
where the time goes in v1:
time: 110 us
  Pallas kernels  100 us (91%)
  local copies, waits for them, and re-layouts  9.08 us (8%)
    pallas_call x1, Pallas kernels, on_device(): pl.pallas_call(functools.partial(kernel, ngx, ngz), out_shape=(jax.ShapeD...  100 us
    unnamed x18, local copies, waits for them, and re-layouts  9.08 us

profile of v1, /device:TPU:1, one launch (start us, length us, event | category | flops | bytes accessed | tf_op | source)
XLA Modules:
  0.0 109.8 jit_solution(12064686093389288523)
XLA Ops:
  0.6 0.0 copy-start
  0.6 1.6 %copy-done = f32[32,64,256]{2,1,0:T(8,128)S(1)} copy-done((f32[32,64,256]{2,1,0:T(8,128)S(1)}, f32[32,64,256]{2,1,0:T(8,128)}, u32[]{:S(2)}) %copy-start) | copy-done | bytes 2097176
  2.2 0.0 copy-start.1
  2.2 1.6 %copy-done.1 = f32[8,256,256]{2,1,0:T(8,128)S(1)} copy-done((f32[8,256,256]{2,1,0:T(8,128)S(1)}, f32[8,256,256]{2,1,0:T(8,128)}, u32[]{:S(2)}) %copy-start.1) | copy-done | bytes 2097176
  3.8 0.0 copy-start.2
  3.8 1.0 copy-done.2
  4.8 0.0 copy-start.3
  4.8 0.8 copy-done.3
  5.6 0.0 copy-start.4
  5.6 0.7 copy-done.4
  6.3 0.0 copy-start.5
  6.3 0.7 copy-done.5
  7.0 0.0 copy-start.6
  7.0 0.7 copy-done.6
  7.7 0.0 copy-start.7
  7.7 0.7 copy-done.7
  8.4 100.0 %rollout.1 = (f32[3,8,32,128]{3,2,1,0:T(8,128)S(1)}, f32[16,8,32]{2,1,0:T(8,128)S(1)}) custom-call(f32[3,8,32,128]{3,2,1,0:T(8,128)S(1)} %copy-done.2, f32[4,8,32]{2,1,0:T(8,128)S(1)} %copy-done.4, f32[256]{0:T(256)S(1)} %copy-done.6, f32[1,128]{1,0:T(1,128)S(1)} %bitcast.1, f32[12,8,32]{2,1,0:T(8,128)S(1)} %copy-done.3, f32[8,32]{1,0:T(8,128)S(1)} %copy-done.5, ...), custom_call_target="tpu_custom_call" | custom-call | tf_op jit(solution)/shard_map/rollout/pallas_call | solution.py:468
  108.4 0.7 copy.12
  109.1 0.6 copy.13
Async XLA Ops:
  0.6 1.6 %copy-start = (f32[32,64,256]{2,1,0:T(8,128)S(1)}, f32[32,64,256]{2,1,0:T(8,128)}, u32[]{:S(2)}) copy-start(f32[32,64,256]{2,1,0:T(8,128)} %constant.5.clone.t2_hbm) | copy-start | bytes 6291460
  2.2 1.6 %copy-start.1 = (f32[8,256,256]{2,1,0:T(8,128)S(1)}, f32[8,256,256]{2,1,0:T(8,128)}, u32[]{:S(2)}) copy-start(f32[8,256,256]{2,1,0:T(8,128)} %constant.4.clone.t1_hbm) | copy-start | bytes 6291460
  3.8 1.0 copy-start.2
  4.8 0.8 copy-start.3
  5.6 0.7 copy-start.4
  6.3 0.7 copy-start.5
  7.0 0.7 copy-start.6
  7.7 0.7 copy-start.7

commit v2 on v1

--- a/solution.py
+++ b/solution.py
@@ -52,15 +52,21 @@
     ngx,
     ngz,
     vel,
+    eddy_hbm,
+    target,
+    mean_hbm,
+    past_hbm,
+    boot_hbm,
+    t1_hbm,
+    t2_hbm,
+    out_vel,
+    out_hbm,
     eddy,
-    target,
     mean,
     past,
     boot,
-    t1_hbm,
-    t2_hbm,
-    out_vel,
     out_ret,
+    fresh,
     field,
     w2,
     w3,
@@ -68,6 +74,8 @@
     nu,
     pack,
     zc,
+    corner_out,
+    corner_in,
     t1,
     t2,
     q_buf,
@@ -96,8 +104,13 @@
     nz = vel.shape[2]
     ny = vel.shape[3]
     span = nz + 2 * HALO
-    rows = (nx + 2 * HALO + 1) * span
+    rows = (nx + 2 * HALO + 3) * span
     past_steps = past.shape[0]
+
+    def each_far(count, send):
+        for step in range(count - 1):
+            away = (step + 1) // 2
+            send(count // 2 + (away if step % 2 else -away), 0)
 
     def xpeer(d):
         return lax.rem(gx + d + ngx, ngx)
@@ -110,9 +123,14 @@
     )
     load_t1 = pltpu.make_async_copy(t1_hbm.at[gz], t1, local_sem.at[1])
     load_t2 = pltpu.make_async_copy(t2_hbm.at[gx], t2, local_sem.at[2])
+    load_eddy = pltpu.make_async_copy(eddy_hbm, eddy, local_sem.at[3])
+    load_mean = pltpu.make_async_copy(mean_hbm, mean, local_sem.at[4])
+    load_past = pltpu.make_async_copy(past_hbm, past, local_sem.at[5])
+    load_boot = pltpu.make_async_copy(boot_hbm, boot, local_sem.at[6])
+    load_eddy.start()
     load_vel.start()
-    load_t1.start()
-    load_t2.start()
+    for load in (load_t1, load_t2, load_mean, load_past, load_boot):
+        load.start()
 
     barrier = pltpu.get_barrier_semaphore()
 
@@ -132,6 +150,7 @@
                 barrier, inc=1, device_id=(xpeer(dx), zpeer(dz)), device_id_type=MESH
             )
 
+    load_eddy.wait()
     eye = (
         lax.broadcasted_iota(jnp.int32, (steps, ny), 0)
         == lax.broadcasted_iota(jnp.int32, (steps, ny), 1)
@@ -145,40 +164,51 @@
             preferred_element_type=jnp.float32,
         )
 
+    first = HALO + 1
+    corners = [(dx, dz) for dx in (1, -1) for dz in (1, -1)]
+
     def halo_copies(s, comps):
         copies = []
-        first = HALO + 1
-        for index, (dx, src, dst) in enumerate(
-            ((1, first + nx - HALO, 1), (-1, first, first + nx))
-        ):
+        for index, (dx, dz) in enumerate(corners):
+            copies.append((corner_out.at[s, index, 0:comps], corner_in.at[s, index, 0:comps], dx, dz))
+        for side, dz in ((0, 1), (1, -1)):
+            copies.append((pack.at[s, side, 0:comps], zc.at[s, side, 0:comps], 0, dz))
+        for dx, src, dst in ((1, first + nx - HALO, 1), (-1, first, first + nx)):
             copies.append(
-                pltpu.make_async_remote_copy(
-                    src_ref=field.at[s, 0:comps, pl.ds(src, HALO), 0:nz, :],
-                    dst_ref=field.at[s, 0:comps, pl.ds(dst, HALO), 0:nz, :],
-                    send_sem=halo_send.at[s, index],
-                    recv_sem=halo_recv.at[s, index],
-                    device_id=(xpeer(dx), gz),
-                    device_id_type=MESH,
+                (
+                    field.at[s, 0:comps, pl.ds(src, HALO), 0:nz, :],
+                    field.at[s, 0:comps, pl.ds(dst, HALO), 0:nz, :],
+                    dx,
+                    0,
                 )
             )
-        for side, dz in ((0, 1), (1, -1)):
-            for index, (dx, src, dst, count) in enumerate(
-                ((0, 0, HALO, nx), (1, nx - HALO, 0, HALO), (-1, 0, HALO + nx, HALO))
-            ):
-                copies.append(
-                    pltpu.make_async_remote_copy(
-                        src_ref=pack.at[s, side, 0:comps, pl.ds(src, count), :, :],
-                        dst_ref=zc.at[s, side, 0:comps, pl.ds(dst, count), :, :],
-                        send_sem=halo_send.at[s, 2 + 3 * side + index],
-                        recv_sem=halo_recv.at[s, 2 + 3 * side + index],
-                        device_id=(xpeer(dx), zpeer(dz)),
-                        device_id_type=MESH,
-                    )
-                )
-        return copies
+        return [
+            pltpu.make_async_remote_copy(
+                src_ref=src,
+                dst_ref=dst,
+                send_sem=halo_send.at[s, index],
+                recv_sem=halo_recv.at[s, index],
+                device_id=(xpeer(dx), zpeer(dz)),
+                device_id_type=MESH,
+            )
+            for index, (src, dst, dx, dz) in enumerate(copies)
+        ]
+
+    diamond = []
+    taken = 0
+    for away in range(1, HALO):
+        diamond.append((away, taken, HALO - away))
+        taken += HALO - away
 
     def start_halo(s, comps):
-        first = HALO + 1
+        for index, (dx, dz) in enumerate(corners):
+            for c in range(comps):
+                for away, at, count in diamond:
+                    line = first + nx - away if dx == 1 else first + away - 1
+                    head = nz - count if dz == 1 else 0
+                    corner_out[s, index, c, at : at + count, :] = field[
+                        s, c, line, head : head + count, :
+                    ]
         for c in range(comps):
             pack[s, 0, c] = field[s, c, pl.ds(first, nx), nz - HALO : nz, :]
             pack[s, 1, c] = field[s, c, pl.ds(first, nx), 0:HALO, :]
@@ -189,10 +219,20 @@
         copies = halo_copies(s, comps)
         for copy in copies:
             copy.wait_recv()
-        total = nx + 2 * HALO
         for c in range(comps):
-            field[s, c, 0:total, nz + HALO : span, :] = zc[s, 0, c]
-            field[s, c, 1 : total + 1, nz : nz + HALO, :] = zc[s, 1, c]
+            field[s, c, pl.ds(first - 1, nx), nz + HALO : span, :] = zc[s, 0, c]
+            field[s, c, pl.ds(first, nx), nz : nz + HALO, :] = zc[s, 1, c]
+        for index, (dx, dz) in enumerate(corners):
+            for c in range(comps):
+                for away, at, count in diamond:
+                    line = first - away if dx == 1 else first + nx - 1 + away
+                    if dz == 1:
+                        line, head = line - 1, span - count
+                    else:
+                        head = nz
+                    field[s, c, line, head : head + count, :] = corner_in[
+                        s, index, c, at : at + count, :
+                    ]
         for copy in copies:
             copy.wait_send()
 
@@ -202,65 +242,79 @@
     rows_y = lane[0:1].astype(jnp.float32) + 0.5
     wall = jnp.minimum(rows_y, ny - rows_y) / (ny / 2.0)
 
-    def tendency(src, nu_s, r):
-        around = [src.at[c, pl.ds(pl.multiple_of(r - 8, 8), 24), :] for c in range(3)]
-        mid = [src[c, pl.ds(pl.multiple_of(r, 8), 8), :] for c in range(3)]
-        visc = nu_s[pl.ds(pl.multiple_of(r, 8), 8), :]
-        hu, hw, hv = mid[0] * 0.5, mid[1] * 0.5, mid[2] * 0.5
+    def here(r):
+        return pl.ds(pl.multiple_of(r, 8), 8)
+
+    def advance(src, nu_s, r, scale, base):
+        mid = [src[c, here(r), :] for c in range(3)]
+        visc = nu_s[here(r), :] * scale
+        half = 0.5 * scale
+        hu, hw, hv = mid[0] * half, mid[1] * half, mid[2] * half
         x_plus, x_minus = visc - hu, visc + hu
         z_plus, z_minus = visc - hw, visc + hw
         y_plus, y_minus = (visc - hv) * mask_plus, (visc + hv) * mask_minus
         center = visc * -6.0
+        if base is None:
+            center = center + 1.0
         out = []
         for c in range(3):
+            around = src.at[c, pl.ds(pl.multiple_of(r - 8, 8), 24), :]
             value = center * mid[c]
-            value += x_plus * src[c, pl.ds(pl.multiple_of(r + span, 8), 8), :]
-            value += x_minus * src[c, pl.ds(pl.multiple_of(r - span, 8), 8), :]
-            value += z_plus * around[c][9:17, :]
-            value += z_minus * around[c][7:15, :]
+            if base is not None:
+                value += base(c, mid[c])
+            if c == 0:
+                value += DRIVE * scale
+            value += x_plus * src[c, here(r + span), :]
+            value += x_minus * src[c, here(r - span), :]
+            value += z_plus * around[9:17, :]
+            value += z_minus * around[7:15, :]
             value += y_plus * pltpu.roll(mid[c], ny - 1, 1)
             value += y_minus * pltpu.roll(mid[c], 1, 1)
-            if c == 0:
-                value += DRIVE
             out.append(value)
-        return mid, out
+        return out
 
     def stages(s):
         v0 = field.at[s].reshape(4, rows, ny)
-        v1 = field.at[s + 1].reshape(4, rows, ny)
         nu_s = nu.at[s].reshape(rows, ny)
-        for k, (src, dst, scale) in enumerate(
-            ((v0, w2, 0.5 * STEP), (w2, w3, 0.5 * STEP), (w3, w4, STEP)), 1
-        ):
-
-            def one(r, src=src, dst=dst, scale=scale):
-                mid, out = tendency(src, nu_s, r)
+        total = nx + 2 * HALO
+
+        def start_value(r):
+            return lambda c, mid: v0[c, here(r), :]
+
+        def last_value(r):
+            return lambda c, mid: (
+                (w2[c, here(r), :] + mid - v0[c, here(r), :]) + 2.0 * w3[c, here(r), :]
+            ) * (1.0 / 3.0)
+
+        plan = (
+            (v0, w2, 0.5 * STEP, lambda r: None),
+            (w2, w3, 0.5 * STEP, start_value),
+            (w3, w4, STEP, start_value),
+            (w4, fresh, STEP / 6.0, last_value),
+        )
+        for k, (src, dst, scale, base) in enumerate(plan, 1):
+            final = k == len(plan)
+            head = k * span + nz + (span - nz if final else 0)
+            tiles = (nz if final else span) // 8
+
+            def one(r, src=src, dst=dst, scale=scale, base=base):
+                out = advance(src, nu_s, r, scale, base(r))
                 for c in range(3):
-                    base = v0[c, pl.ds(pl.multiple_of(r, 8), 8), :]
-                    dst[c, pl.ds(pl.multiple_of(r, 8), 8), :] = base + scale * out[c]
-
-            def line(i, carry, k=k, one=one):
-                start = k * span + nz + i * span
-                for t in range(span // 8):
-                    one(start + 8 * t)
-                return carry
-
-            total = nx + 2 * HALO
-            lax.fori_loop(0, total - 2 * k, line, 0)
-            one((total + 1 - k) * span - 8)
-
-        def last(i, carry):
-            start = (HALO + 1 + i) * span
-            for t in range(nz // 8):
-                r = start + 8 * t
-                here = pl.ds(pl.multiple_of(r, 8), 8)
-                mid, out = tendency(w4, nu_s, r)
-                for c in range(3):
-                    mean_part = (w2[c, here, :] + mid[c] - v0[c, here, :]) + 2.0 * w3[c, here, :]
-                    v1[c, here, :] = mean_part * (1.0 / 3.0) + (STEP / 6.0) * out[c]
-            return carry
-
-        lax.fori_loop(0, nx, last, 0)
+                    dst[c, here(r), :] = out[c]
+
+            def line(i, carry, one=one, head=head, tiles=tiles):
+                def tile(t, inner):
+                    one(head + i * span + 8 * t)
+                    return inner
+
+                return lax.fori_loop(0, tiles, tile, carry, unroll=True)
+
+            lax.fori_loop(0, total - 2 * k, line, 0, unroll=True)
+            if not final:
+                one((total + 1 - k) * span - 8)
+        for c in range(3):
+            for x in range(nx):
+                field[s + 1, c, first + x, 0:nz, :] = fresh[c, pl.ds((first + x) * span, nz), :]
 
     def interior(s, c):
         return field[s, c, pl.ds(HALO + 1, nx), 0:nz, :]
@@ -283,7 +337,7 @@
             ).start()
             return carry
 
-        lax.fori_loop(1, ngz, send, 0)
+        each_far(ngz, send)
         r_buf[s, ngz - 1] = q_buf[s, gz]
 
     def wait_bytes(ref, sem):
@@ -311,7 +365,7 @@
             ).start()
             return carry
 
-        lax.fori_loop(1, ngx, send, 0)
+        each_far(ngx, send)
         s_buf[s, ngx - 1] = p_buf[s, gx]
 
     def finish_gx(s):
@@ -346,17 +400,18 @@
     load_vel.wait()
     pl.semaphore_wait(barrier, ngx + ngz + 2)
     start_halo(0, 4)
-    load_t1.wait()
-    load_t2.wait()
+    for load in (load_t1, load_t2, load_mean, load_past, load_boot):
+        load.wait()
     wait_halo(0, 4)
 
-    def viscosity(i, carry):
-        each = field[0, 3, i]
-        for s in range(steps):
-            nu[s, i] = BASE_VISCOSITY + each[:, s : s + 1] * wall
-        return carry
-
-    lax.fori_loop(0, nx + 2 * HALO + 1, viscosity, 0)
+    def viscosity(s):
+        def each(i, carry):
+            nu[s, i] = BASE_VISCOSITY + field[0, 3, i][:, s : s + 1] * wall
+            return carry
+
+        lax.fori_loop(0, nx + 2 * HALO + 1, each, 0)
+
+    viscosity(0)
 
     def body(s, carry):
         stages(s)
@@ -367,6 +422,8 @@
 
         start_gz(s)
         local_reward(s)
+        for later in range(1, steps):
+            pl.when(s == later - 1)(functools.partial(viscosity, later))
 
         @pl.when(s >= 1)
         def _():
@@ -411,7 +468,7 @@
         ).start()
         return carry
 
-    lax.fori_loop(1, ngx, send_x, 0)
+    each_far(ngx, send_x)
     wait_bytes(a_buf, ar_recv.at[0])
     b_tile[...] = term[...] + jnp.sum(a_buf[...], axis=0)
 
@@ -426,7 +483,7 @@
         ).start()
         return carry
 
-    lax.fori_loop(1, ngz, send_z, 0)
+    each_far(ngz, send_z)
     wait_bytes(b_buf, ar_recv.at[1])
     spectrum = (b_tile[...] + jnp.sum(b_buf[...], axis=0)) * (-1.0 / KX)
 
@@ -438,6 +495,8 @@
             new = spectrum[t - past_steps : t - past_steps + 1, 0:nz]
             extra = new if extra is None else extra + new
         out_ret[t] = plain[t] + extra
+    store_ret = pltpu.make_async_copy(out_ret, out_hbm, local_sem.at[1])
+    store_ret.start()
 
     def drain(s, carry):
         wait_bytes(r_buf.at[s, 0 : ngz - 1], gz_send.at[s])
@@ -448,6 +507,12 @@
     wait_bytes(a_buf, ar_send.at[0])
     wait_bytes(b_buf, ar_send.at[1])
     store_vel.wait()
+    store_ret.wait()
+
+
+def place(vel, ret, out_vel, out_ret):
+    out_vel[...] = vel[...]
+    out_ret[...] = ret[...]
 
 
 def on_device(
@@ -459,28 +524,36 @@
     t1 = z_table(ngz, nx, nz, nx * ngx, nz * ngz)
     t2 = x_table(ngx, ngz, nx, nx * ngx)
     span = nz + 2 * HALO
-    lines = nx + 2 * HALO + 1
+    lines = nx + 2 * HALO + 3
     f32 = jnp.float32
-    vmem = pl.BlockSpec(memory_space=pltpu.VMEM)
-    hbm = pl.BlockSpec(memory_space=pl.ANY)
+    hbm = pl.BlockSpec(memory_space=pltpu.HBM)
+    free = pl.BlockSpec(memory_space=pl.ANY)
     smem = pl.BlockSpec(memory_space=pltpu.SMEM)
     dma = pltpu.SemaphoreType.DMA
-    return pl.pallas_call(
+    found = pl.pallas_call(
         functools.partial(kernel, ngx, ngz),
         out_shape=(
             jax.ShapeDtypeStruct(velocity.shape, f32),
             jax.ShapeDtypeStruct((horizon, nx, nz), f32),
         ),
-        in_specs=[hbm, vmem, smem, vmem, vmem, vmem, hbm, hbm],
-        out_specs=(hbm, vmem),
+        in_specs=[hbm, hbm, smem, hbm, hbm, hbm, hbm, hbm],
+        out_specs=(free, free),
         scratch_shapes=[
+            pltpu.VMEM(eddy_viscosity.shape, f32),
+            pltpu.VMEM((1, ny), f32),
+            pltpu.VMEM(past_rewards.shape, f32),
+            pltpu.VMEM(bootstrap_values.shape, f32),
+            pltpu.VMEM((horizon, nx, nz), f32),
+            pltpu.VMEM((3, lines * span, ny), f32),
             pltpu.VMEM((steps + 1, 4, lines, span, ny), f32),
             pltpu.VMEM((3, lines * span, ny), f32),
             pltpu.VMEM((3, lines * span, ny), f32),
             pltpu.VMEM((3, lines * span, ny), f32),
             pltpu.VMEM((steps, lines, span, ny), f32),
             pltpu.VMEM((steps, 2, 4, nx, HALO, ny), f32),
-            pltpu.VMEM((steps, 2, 4, nx + 2 * HALO, HALO, ny), f32),
+            pltpu.VMEM((steps, 2, 4, nx, HALO, ny), f32),
+            pltpu.VMEM((steps, 4, 4, 8, ny), f32),
+            pltpu.VMEM((steps, 4, 4, 8, ny), f32),
             pltpu.VMEM(t1.shape[1:], f32),
             pltpu.VMEM(t2.shape[1:], f32),
             pltpu.VMEM((steps, ngz, 3, t1.shape[1] // ngz, ny), f32),
@@ -492,7 +565,7 @@
             pltpu.VMEM((ngx - 1, 8, ny), f32),
             pltpu.VMEM((8, ny), f32),
             pltpu.VMEM((ngz - 1, 8, ny), f32),
-            dma((3,)),
+            dma((7,)),
             dma((steps, 8)),
             dma((steps, 8)),
             dma((steps,)),
@@ -503,7 +576,7 @@
             dma((2,)),
         ],
         compiler_params=pltpu.CompilerParams(
-            collective_id=0, has_side_effects=True, vmem_limit_bytes=48 * 1024 * 1024
+            collective_id=0, has_side_effects=True, vmem_limit_bytes=62 * 1024 * 1024
         ),
         name="rollout",
     )(
@@ -516,6 +589,14 @@
         jnp.asarray(t1),
         jnp.asarray(t2),
     )
+
+    return pl.pallas_call(
+        place,
+        out_shape=tuple(jax.ShapeDtypeStruct(part.shape, f32) for part in found),
+        in_specs=[pl.BlockSpec(memory_space=pltpu.VMEM)] * 2,
+        out_specs=(pl.BlockSpec(memory_space=pltpu.VMEM),) * 2,
+        name="place",
+    )(*found)
 
 
 def solution(mesh):

time: 110 us -> 86.4 us (0.79)
  Pallas kernels: 100 us -> 85.6 us
  local copies, waits for them, and re-layouts: 9.08 us -> 0 us
    pallas_call x1, Pallas kernels: 100 us -> 83.8 us  [on_device(): pl.pallas_call(functools.partial(kernel, ngx, ngz), out_shape=(jax.ShapeD...]
    unnamed x18 -> x0, local copies, waits for them, and re-layouts: 9.08 us -> none
    pallas_call x0 -> x1, Pallas kernels: none -> 1.78 us  [on_device(): pl.pallas_call(place, out_shape=tuple((jax.ShapeDtypeStruct(part.shape, f...]
where the time goes in v2:
time: 86.4 us; the launch traced here: 86.2 us
  Pallas kernels  85.6 us (99%)
    pallas_call x1, Pallas kernels, on_device(): pl.pallas_call(functools.partial(kernel, ngx, ngz), out_shape=(jax.ShapeD...  83.8 us
    pallas_call x1, Pallas kernels, on_device(): pl.pallas_call(place, out_shape=tuple((jax.ShapeDtypeStruct(part.shape, f...  1.78 us

profile of v2, /device:TPU:1, one launch (start us, length us, event | category | flops | bytes accessed | tf_op | source)
XLA Modules:
  0.0 86.2 jit_solution(10875877208039246287)
XLA Ops:
  0.6 83.8 %rollout.1 = (f32[3,8,32,128]{3,2,1,0:T(8,128)}, f32[16,8,32]{2,1,0:T(8,128)}) custom-call(f32[3,8,32,128]{3,2,1,0:T(8,128)} %vel.1, f32[4,8,32]{2,1,0:T(8,128)} %eddy_hbm.1, f32[256]{0:T(256)} %target.1, f32[1,128]{1,0:T(1,128)} %bitcast.1, f32[12,8,32]{2,1,0:T(8,128)} %past_hbm.1, f32[8,32]{1,0:T(8,128)} %boot_hbm.1, f32[8,256,256]{2,1,0:T(8,128)} %constant.4.clone.t1_hbm, ...), custom_call_target="tpu_custom_call" | custom-call | tf_op jit(solution)/shard_map/rollout/pallas_call | solution.py:533
  84.4 1.8 %place.1 = (f32[3,8,32,128]{3,2,1,0:T(8,128)}, f32[16,8,32]{2,1,0:T(8,128)}) custom-call(f32[3,8,32,128]{3,2,1,0:T(8,128)} %get-tuple-element.4.vel, f32[16,8,32]{2,1,0:T(8,128)} %get-tuple-element.5.ret), custom_call_target="tpu_custom_call" | custom-call | tf_op jit(solution)/shard_map/place/pallas_call | solution.py:593

commit v3 on v2

--- a/solution.py
+++ b/solution.py
@@ -215,9 +215,12 @@
         for copy in halo_copies(s, comps):
             copy.start()
 
-    def wait_halo(s, comps):
-        copies = halo_copies(s, comps)
-        for copy in copies:
+    def wait_x(s, comps):
+        for copy in halo_copies(s, comps)[6:]:
+            copy.wait_recv()
+
+    def wait_z(s, comps):
+        for copy in halo_copies(s, comps)[:6]:
             copy.wait_recv()
         for c in range(comps):
             field[s, c, pl.ds(first - 1, nx), nz + HALO : span, :] = zc[s, 0, c]
@@ -233,7 +236,9 @@
                     field[s, c, line, head : head + count, :] = corner_in[
                         s, index, c, at : at + count, :
                     ]
-        for copy in copies:
+
+    def wait_sent(s, comps):
+        for copy in halo_copies(s, comps):
             copy.wait_send()
 
     lane = lax.broadcasted_iota(jnp.int32, (8, ny), 1)
@@ -273,7 +278,7 @@
             out.append(value)
         return out
 
-    def stages(s):
+    def stages(s, inner):
         v0 = field.at[s].reshape(4, rows, ny)
         nu_s = nu.at[s].reshape(rows, ny)
         total = nx + 2 * HALO
@@ -294,24 +299,26 @@
         )
         for k, (src, dst, scale, base) in enumerate(plan, 1):
             final = k == len(plan)
-            head = k * span + nz + (span - nz if final else 0)
-            tiles = (nz if final else span) // 8
+            if inner:
+                tiles = range(8, nz - 8, 8) if final else range(0, nz, 8)
+            else:
+                tiles = (0, nz - 8) if final else (-8, 0, nz - 8)
 
             def one(r, src=src, dst=dst, scale=scale, base=base):
                 out = advance(src, nu_s, r, scale, base(r))
                 for c in range(3):
                     dst[c, here(r), :] = out[c]
 
-            def line(i, carry, one=one, head=head, tiles=tiles):
-                def tile(t, inner):
-                    one(head + i * span + 8 * t)
-                    return inner
-
-                return lax.fori_loop(0, tiles, tile, carry, unroll=True)
+            def line(i, carry, k=k, one=one, tiles=tiles):
+                for t in tiles:
+                    one((k + 1 + i) * span + t)
+                return carry
 
             lax.fori_loop(0, total - 2 * k, line, 0, unroll=True)
-            if not final:
+            if not inner and not final:
                 one((total + 1 - k) * span - 8)
+
+    def settle(s):
         for c in range(3):
             for x in range(nx):
                 field[s + 1, c, first + x, 0:nz, :] = fresh[c, pl.ds((first + x) * span, nz), :]
@@ -402,19 +409,32 @@
     start_halo(0, 4)
     for load in (load_t1, load_t2, load_mean, load_past, load_boot):
         load.wait()
-    wait_halo(0, 4)
-
-    def viscosity(s):
+
+    def viscosity(s, head, end):
         def each(i, carry):
-            nu[s, i] = BASE_VISCOSITY + field[0, 3, i][:, s : s + 1] * wall
+            part = field[0, 3, i, head:end, :]
+            nu[s, i, head:end, :] = BASE_VISCOSITY + part[:, s : s + 1] * wall
             return carry
 
         lax.fori_loop(0, nx + 2 * HALO + 1, each, 0)
 
-    viscosity(0)
+    wait_x(0, 4)
+    viscosity(0, 0, nz)
 
     def body(s, carry):
-        stages(s)
+        stages(s, True)
+
+        @pl.when(s == 0)
+        def _():
+            wait_z(0, 4)
+            viscosity(0, nz, span)
+
+        @pl.when(s >= 1)
+        def _():
+            wait_z(s, 3)
+
+        stages(s, False)
+        settle(s)
 
         @pl.when(s < steps - 1)
         def _():
@@ -423,7 +443,7 @@
         start_gz(s)
         local_reward(s)
         for later in range(1, steps):
-            pl.when(s == later - 1)(functools.partial(viscosity, later))
+            pl.when(s == later - 1)(functools.partial(viscosity, later, 0, span))
 
         @pl.when(s >= 1)
         def _():
@@ -435,7 +455,7 @@
 
         @pl.when(s < steps - 1)
         def _():
-            wait_halo(s + 1, 3)
+            wait_x(s + 1, 3)
 
         return carry
 
@@ -445,8 +465,8 @@
         field.at[steps, 0:3, pl.ds(HALO + 1, nx), 0:nz, :], out_vel, local_sem.at[0]
     )
     store_vel.start()
+    start_gx(steps - 1)
     finish_gx(steps - 2)
-    start_gx(steps - 1)
 
     plain = [None] * (past_steps + steps)
     running = boot[...]
@@ -504,6 +524,9 @@
         return carry
 
     lax.fori_loop(0, steps, drain, 0)
+    wait_sent(0, 4)
+    for s in range(1, steps):
+        wait_sent(s, 3)
     wait_bytes(a_buf, ar_send.at[0])
     wait_bytes(b_buf, ar_send.at[1])
     store_vel.wait()

time: 86.4 us -> 82.3 us (0.953)
  Pallas kernels: 85.6 us -> 81.4 us
    pallas_call x1, Pallas kernels: 83.8 us -> 79.7 us  [on_device(): pl.pallas_call(functools.partial(kernel, ngx, ngz), out_shape=(jax.ShapeD...]
where the time goes in v3:
time: 82.3 us; the launch traced here: 82.1 us
  Pallas kernels  81.4 us (99%)
    pallas_call x1, Pallas kernels, on_device(): pl.pallas_call(functools.partial(kernel, ngx, ngz), out_shape=(jax.ShapeD...  79.7 us
    pallas_call x1, Pallas kernels, on_device(): pl.pallas_call(place, out_shape=tuple((jax.ShapeDtypeStruct(part.shape, f...  1.78 us

profile of v3, /device:TPU:1, one launch (start us, length us, event | category | flops | bytes accessed | tf_op | source)
XLA Modules:
  0.0 82.1 jit_solution(774511610100029517)
XLA Ops:
  0.6 79.7 %rollout.1 = (f32[3,8,32,128]{3,2,1,0:T(8,128)}, f32[16,8,32]{2,1,0:T(8,128)}) custom-call(f32[3,8,32,128]{3,2,1,0:T(8,128)} %vel.1, f32[4,8,32]{2,1,0:T(8,128)} %eddy_hbm.1, f32[256]{0:T(256)} %target.1, f32[1,128]{1,0:T(1,128)} %bitcast.1, f32[12,8,32]{2,1,0:T(8,128)} %past_hbm.1, f32[8,32]{1,0:T(8,128)} %boot_hbm.1, f32[8,256,256]{2,1,0:T(8,128)} %constant.4.clone.t1_hbm, ...), custom_call_target="tpu_custom_call" | custom-call | tf_op jit(solution)/shard_map/rollout/pallas_call | solution.py:556
  80.3 1.8 %place.1 = (f32[3,8,32,128]{3,2,1,0:T(8,128)}, f32[16,8,32]{2,1,0:T(8,128)}) custom-call(f32[3,8,32,128]{3,2,1,0:T(8,128)} %get-tuple-element.4.vel, f32[16,8,32]{2,1,0:T(8,128)} %get-tuple-element.5.ret), custom_call_target="tpu_custom_call" | custom-call | tf_op jit(solution)/shard_map/place/pallas_call | solution.py:616

commit v4 on v3

--- a/solution.py
+++ b/solution.py
@@ -118,6 +118,24 @@
     def zpeer(d):
         return lax.rem(gz + d + ngz, ngz)
 
+    barrier = pltpu.get_barrier_semaphore()
+
+    def greet_x(d, carry):
+        pl.semaphore_signal(barrier, inc=1, device_id=(xpeer(d), gz), device_id_type=MESH)
+        return carry
+
+    def greet_z(d, carry):
+        pl.semaphore_signal(barrier, inc=1, device_id=(gx, zpeer(d)), device_id_type=MESH)
+        return carry
+
+    each_far(ngx, greet_x)
+    each_far(ngz, greet_z)
+    for dx in (-1, 1):
+        for dz in (-1, 1):
+            pl.semaphore_signal(
+                barrier, inc=1, device_id=(xpeer(dx), zpeer(dz)), device_id_type=MESH
+            )
+
     load_vel = pltpu.make_async_copy(
         vel, field.at[0, 0:3, pl.ds(HALO + 1, nx), 0:nz, :], local_sem.at[0]
     )
@@ -131,24 +149,6 @@
     load_vel.start()
     for load in (load_t1, load_t2, load_mean, load_past, load_boot):
         load.start()
-
-    barrier = pltpu.get_barrier_semaphore()
-
-    def greet_x(d, carry):
-        pl.semaphore_signal(barrier, inc=1, device_id=(xpeer(d), gz), device_id_type=MESH)
-        return carry
-
-    def greet_z(d, carry):
-        pl.semaphore_signal(barrier, inc=1, device_id=(gx, zpeer(d)), device_id_type=MESH)
-        return carry
-
-    lax.fori_loop(1, ngx, greet_x, 0)
-    lax.fori_loop(1, ngz, greet_z, 0)
-    for dx in (-1, 1):
-        for dz in (-1, 1):
-            pl.semaphore_signal(
-                barrier, inc=1, device_id=(xpeer(dx), zpeer(dz)), device_id_type=MESH
-            )
 
     load_eddy.wait()
     eye = (
@@ -200,19 +200,23 @@
         diamond.append((away, taken, HALO - away))
         taken += HALO - away
 
-    def start_halo(s, comps):
+    def start_edges(s, comps, source):
         for index, (dx, dz) in enumerate(corners):
             for c in range(comps):
                 for away, at, count in diamond:
                     line = first + nx - away if dx == 1 else first + away - 1
                     head = nz - count if dz == 1 else 0
-                    corner_out[s, index, c, at : at + count, :] = field[
-                        s, c, line, head : head + count, :
+                    corner_out[s, index, c, at : at + count, :] = source[
+                        c, line, head : head + count, :
                     ]
         for c in range(comps):
-            pack[s, 0, c] = field[s, c, pl.ds(first, nx), nz - HALO : nz, :]
-            pack[s, 1, c] = field[s, c, pl.ds(first, nx), 0:HALO, :]
-        for copy in halo_copies(s, comps):
+            pack[s, 0, c] = source[c, pl.ds(first, nx), nz - HALO : nz, :]
+            pack[s, 1, c] = source[c, pl.ds(first, nx), 0:HALO, :]
+        for copy in halo_copies(s, comps)[:6]:
+            copy.start()
+
+    def start_lines(s, comps):
+        for copy in halo_copies(s, comps)[6:]:
             copy.start()
 
     def wait_x(s, comps):
@@ -352,14 +356,11 @@
 
     def start_gx(s):
         wait_bytes(r_buf.at[s, 0 : ngz - 1], gz_recv.at[s])
-        p_flat = p_buf.at[s].reshape(ngx * 8, ny)
         for c in range(3):
             value = r_buf[s, :, c].reshape(t2.shape[1], ny)
             part = jnp.dot(t2[...], value, precision=HIGH, preferred_element_type=jnp.float32)
             for q in range(2):
-                p_flat[pl.ds(2 * c + q, ngx, stride=8), :] = part[q * ngx : (q + 1) * ngx]
-        for q in (6, 7):
-            p_flat[pl.ds(q, ngx, stride=8), :] = jnp.zeros((ngx, ny), jnp.float32)
+                p_buf[s, :, c, q, :] = part[q * ngx : (q + 1) * ngx]
 
         def send(d, carry):
             pltpu.make_async_remote_copy(
@@ -378,13 +379,13 @@
     def finish_gx(s):
         wait_bytes(s_buf.at[s, 0 : ngx - 1], gx_recv.at[s])
         coefs = jnp.sum(s_buf[s], axis=0)
-        energy = jnp.sum(coefs * coefs) * (1.0 / ny)
+        energy = jnp.sum(jnp.sum(coefs * coefs, axis=0), axis=(0, 1), keepdims=True) * (1.0 / ny)
         own = KZ // ngz
         wave = (gx // own) * KZ + gz * own + lax.rem(gx, own)
-        energy = jnp.full((1, ny), energy, jnp.float32)
+        energy = jnp.broadcast_to(energy, (1, ny))
         goal = jnp.full((1, ny), target[wave], jnp.float32)
         ratio = (energy - goal) / (energy + goal)
-        term[pl.ds(s, 1), :] = ratio * ratio
+        term[...] += jnp.where(lane[0:1] == s, ratio * ratio, 0.0)
 
     def local_reward(s):
         offset = interior(s + 1, 0) - mean[...].reshape(1, 1, ny)
@@ -406,7 +407,8 @@
     term[...] = jnp.zeros_like(term)
     load_vel.wait()
     pl.semaphore_wait(barrier, ngx + ngz + 2)
-    start_halo(0, 4)
+    start_edges(0, 4, field.at[0])
+    start_lines(0, 4)
     for load in (load_t1, load_t2, load_mean, load_past, load_boot):
         load.wait()
 
@@ -434,11 +436,16 @@
             wait_z(s, 3)
 
         stages(s, False)
-        settle(s)
 
         @pl.when(s < steps - 1)
         def _():
-            start_halo(s + 1, 3)
+            start_edges(s + 1, 3, fresh.reshape(3, rows // span, span, ny))
+
+        settle(s)
+
+        @pl.when(s < steps - 1)
+        def _():
+            start_lines(s + 1, 3)
 
         start_gz(s)
         local_reward(s)
@@ -512,7 +519,7 @@
         if extra is not None:
             extra = extra * DISCOUNT
         if t >= past_steps:
-            new = spectrum[t - past_steps : t - past_steps + 1, 0:nz]
+            new = spectrum[:, t - past_steps : t - past_steps + 1]
             extra = new if extra is None else extra + new
         out_ret[t] = plain[t] + extra
     store_ret = pltpu.make_async_copy(out_ret, out_hbm, local_sem.at[1])
@@ -581,13 +588,13 @@
             pltpu.VMEM(t2.shape[1:], f32),
             pltpu.VMEM((steps, ngz, 3, t1.shape[1] // ngz, ny), f32),
             pltpu.VMEM((steps, ngz, 3, t1.shape[1] // ngz, ny), f32),
-            pltpu.VMEM((steps, ngx, 8, ny), f32),
-            pltpu.VMEM((steps, ngx, 8, ny), f32),
+            pltpu.VMEM((steps, ngx, 3, 2, ny), f32),
+            pltpu.VMEM((steps, ngx, 3, 2, ny), f32),
             pltpu.VMEM((steps, nx, nz), f32),
-            pltpu.VMEM((8, ny), f32),
-            pltpu.VMEM((ngx - 1, 8, ny), f32),
-            pltpu.VMEM((8, ny), f32),
-            pltpu.VMEM((ngz - 1, 8, ny), f32),
+            pltpu.VMEM((1, ny), f32),
+            pltpu.VMEM((ngx - 1, 1, ny), f32),
+            pltpu.VMEM((1, ny), f32),
+            pltpu.VMEM((ngz - 1, 1, ny), f32),
             dma((7,)),
             dma((steps, 8)),
             dma((steps, 8)),

time: 82.3 us -> 80.8 us (0.982)
  Pallas kernels: 81.4 us -> 80 us
    pallas_call x1, Pallas kernels: 79.7 us -> 78.2 us  [on_device(): pl.pallas_call(functools.partial(kernel, ngx, ngz), out_shape=(jax.ShapeD...]
where the time goes in v4:
time: 80.8 us; the launch traced here: 80.6 us
  Pallas kernels  80 us (99%)
    pallas_call x1, Pallas kernels, on_device(): pl.pallas_call(functools.partial(kernel, ngx, ngz), out_shape=(jax.ShapeD...  78.2 us
    pallas_call x1, Pallas kernels, on_device(): pl.pallas_call(place, out_shape=tuple((jax.ShapeDtypeStruct(part.shape, f...  1.78 us

profile of v4, /device:TPU:1, one launch (start us, length us, event | category | flops | bytes accessed | tf_op | source)
XLA Modules:
  0.0 80.6 jit_solution(1520034519841255995)
XLA Ops:
  0.6 78.2 %rollout.1 = (f32[3,8,32,128]{3,2,1,0:T(8,128)}, f32[16,8,32]{2,1,0:T(8,128)}) custom-call(f32[3,8,32,128]{3,2,1,0:T(8,128)} %vel.1, f32[4,8,32]{2,1,0:T(8,128)} %eddy_hbm.1, f32[256]{0:T(256)} %target.1, f32[1,128]{1,0:T(1,128)} %bitcast.1, f32[12,8,32]{2,1,0:T(8,128)} %past_hbm.1, f32[8,32]{1,0:T(8,128)} %boot_hbm.1, f32[8,256,256]{2,1,0:T(8,128)} %constant.4.clone.t1_hbm, ...), custom_call_target="tpu_custom_call" | custom-call | tf_op jit(solution)/shard_map/rollout/pallas_call | solution.py:563
  78.8 1.8 %place.1 = (f32[3,8,32,128]{3,2,1,0:T(8,128)}, f32[16,8,32]{2,1,0:T(8,128)}) custom-call(f32[3,8,32,128]{3,2,1,0:T(8,128)} %get-tuple-element.4.vel, f32[16,8,32]{2,1,0:T(8,128)} %get-tuple-element.5.ret), custom_call_target="tpu_custom_call" | custom-call | tf_op jit(solution)/shard_map/place/pallas_call | solution.py:623

commit v5 on v4

--- a/solution.py
+++ b/solution.py
@@ -168,6 +168,7 @@
     corners = [(dx, dz) for dx in (1, -1) for dz in (1, -1)]
 
     def halo_copies(s, comps):
+        source = field.at[0] if comps == 4 else fresh
         copies = []
         for index, (dx, dz) in enumerate(corners):
             copies.append((corner_out.at[s, index, 0:comps], corner_in.at[s, index, 0:comps], dx, dz))
@@ -176,7 +177,7 @@
         for dx, src, dst in ((1, first + nx - HALO, 1), (-1, first, first + nx)):
             copies.append(
                 (
-                    field.at[s, 0:comps, pl.ds(src, HALO), 0:nz, :],
+                    source.at[0:comps, pl.ds(src, HALO), 0:nz, :],
                     field.at[s, 0:comps, pl.ds(dst, HALO), 0:nz, :],
                     dx,
                     0,
@@ -222,6 +223,7 @@
     def wait_x(s, comps):
         for copy in halo_copies(s, comps)[6:]:
             copy.wait_recv()
+            copy.wait_send()
 
     def wait_z(s, comps):
         for copy in halo_copies(s, comps)[:6]:
@@ -242,7 +244,7 @@
                     ]
 
     def wait_sent(s, comps):
-        for copy in halo_copies(s, comps):
+        for copy in halo_copies(s, comps)[:6]:
             copy.wait_send()
 
     lane = lax.broadcasted_iota(jnp.int32, (8, ny), 1)
@@ -299,7 +301,7 @@
             (v0, w2, 0.5 * STEP, lambda r: None),
             (w2, w3, 0.5 * STEP, start_value),
             (w3, w4, STEP, start_value),
-            (w4, fresh, STEP / 6.0, last_value),
+            (w4, fresh.reshape(3, rows, ny), STEP / 6.0, last_value),
         )
         for k, (src, dst, scale, base) in enumerate(plan, 1):
             final = k == len(plan)
@@ -325,7 +327,7 @@
     def settle(s):
         for c in range(3):
             for x in range(nx):
-                field[s + 1, c, first + x, 0:nz, :] = fresh[c, pl.ds((first + x) * span, nz), :]
+                field[s + 1, c, first + x, 0:nz, :] = fresh[c, first + x, 0:nz, :]
 
     def interior(s, c):
         return field[s, c, pl.ds(HALO + 1, nx), 0:nz, :]
@@ -333,7 +335,7 @@
     def start_gz(s):
         cells = nx * nz
         for c in range(3):
-            value = interior(s + 1, c).reshape(cells, ny)
+            value = fresh[c, pl.ds(first, nx), 0:nz, :].reshape(cells, ny)
             part = jnp.dot(t1[...], value, precision=HIGH, preferred_element_type=jnp.float32)
             q_buf[s, :, c] = part.reshape(ngz, part.shape[0] // ngz, ny)
 
@@ -439,15 +441,11 @@
 
         @pl.when(s < steps - 1)
         def _():
-            start_edges(s + 1, 3, fresh.reshape(3, rows // span, span, ny))
-
+            start_edges(s + 1, 3, fresh)
+            start_lines(s + 1, 3)
+
+        start_gz(s)
         settle(s)
-
-        @pl.when(s < steps - 1)
-        def _():
-            start_lines(s + 1, 3)
-
-        start_gz(s)
         local_reward(s)
         for later in range(1, steps):
             pl.when(s == later - 1)(functools.partial(viscosity, later, 0, span))
@@ -574,7 +572,7 @@
             pltpu.VMEM(past_rewards.shape, f32),
             pltpu.VMEM(bootstrap_values.shape, f32),
             pltpu.VMEM((horizon, nx, nz), f32),
-            pltpu.VMEM((3, lines * span, ny), f32),
+            pltpu.VMEM((3, lines, span, ny), f32),
             pltpu.VMEM((steps + 1, 4, lines, span, ny), f32),
             pltpu.VMEM((3, lines * span, ny), f32),
             pltpu.VMEM((3, lines * span, ny), f32),

time: 80.8 us -> 80.7 us (level)
  no operation moved by 1% of the time
where the time goes in v5:
time: 80.7 us; the launch traced here: 80.5 us
  Pallas kernels  79.9 us (99%)
    pallas_call x1, Pallas kernels, on_device(): pl.pallas_call(functools.partial(kernel, ngx, ngz), out_shape=(jax.ShapeD...  78.1 us
    pallas_call x1, Pallas kernels, on_device(): pl.pallas_call(place, out_shape=tuple((jax.ShapeDtypeStruct(part.shape, f...  1.78 us

profile of v5, /device:TPU:1, one launch (start us, length us, event | category | flops | bytes accessed | tf_op | source)
XLA Modules:
  0.0 80.5 jit_solution(1104850769211474639)
XLA Ops:
  0.6 78.1 %rollout.1 = (f32[3,8,32,128]{3,2,1,0:T(8,128)}, f32[16,8,32]{2,1,0:T(8,128)}) custom-call(f32[3,8,32,128]{3,2,1,0:T(8,128)} %vel.1, f32[4,8,32]{2,1,0:T(8,128)} %eddy_hbm.1, f32[256]{0:T(256)} %target.1, f32[1,128]{1,0:T(1,128)} %bitcast.1, f32[12,8,32]{2,1,0:T(8,128)} %past_hbm.1, f32[8,32]{1,0:T(8,128)} %boot_hbm.1, f32[8,256,256]{2,1,0:T(8,128)} %constant.4.clone.t1_hbm, ...), custom_call_target="tpu_custom_call" | custom-call | tf_op jit(solution)/shard_map/rollout/pallas_call | solution.py:561
  78.7 1.8 %place.1 = (f32[3,8,32,128]{3,2,1,0:T(8,128)}, f32[16,8,32]{2,1,0:T(8,128)}) custom-call(f32[3,8,32,128]{3,2,1,0:T(8,128)} %get-tuple-element.4.vel, f32[16,8,32]{2,1,0:T(8,128)} %get-tuple-element.5.ret), custom_call_target="tpu_custom_call" | custom-call | tf_op jit(solution)/shard_map/place/pallas_call | solution.py:621
